TPU v7x, 256 devices: a whole 4x4x8 slice. The times are simulated.
256 devices in a mesh: ctx: 64 (over y, z, core), head: 4 (over x).
Axes of the slice: x: 4, y: 4, z: 8, core: 2. Of those that a mesh axis runs over, the one named last changes fastest.
Arguments:
- queries: bfloat16 [32768, 2048], P('ctx', 'head'), may hold values from -8 to 8
- keys: bfloat16 [32768, 128], P('ctx'), may hold values from -8 to 8
- values: bfloat16 [32768, 128], P('ctx'), may hold values from -6 to 6
- out_grad: bfloat16 [32768, 2048], P('ctx', 'head'), may hold values from -6 to 6
- doc_start: int32 [32768], P('ctx'), may hold values from 0 to 32767, as said below
- block_seq: int32 [64], replicated, may hold values from 0 to 63, as said below
Outputs:
- query_grad: bfloat16 [32768, 2048], P('ctx', 'head')
- key_grad: bfloat16 [32768, 128], P(('ctx', 'head'))
- value_grad: bfloat16 [32768, 128], P(('ctx', 'head'))
Inputs may be any that keep to these rules, and one draw needn't show every extreme that they name: Position d along ctx holds sequence block block_seq[d]; block_seq is a permutation that maps each aligned pair of positions 2k and 2k + 1 onto itself. doc_start of a stored row is the sequence position of the first token of that row's document, at most the row's own position; documents are runs of consecutive positions of at most 1024 tokens, and one document has exactly 1024 tokens.
All inputs are finite; a program needn't handle non-finite values.
Results may differ from a plain program's by a relative error of at most 0.015.
Values may be sent and summed in bfloat16 or wider, within the bound.
A program may use at most 64 MiB of HBM per device.

v0:
```python
import jax
import jax.numpy as jnp
from jax import lax
from jax.sharding import PartitionSpec as P


def passed_along(block, axis, distance):
    devices = range(lax.axis_size(axis))
    route = [(i - distance, i) for i in devices if i - distance in devices]
    return lax.ppermute(block, axis, route)


def contract_rows(left_side, right_side, left_axis, right_axis):
    return lax.dot_general(
        left_side,
        right_side,
        (((left_axis,), (right_axis,)), ((), ())),
        preferred_element_type=jnp.float32,
    )


def shards(queries, keys, values, out_grad, doc_start, block_seq):
    row_count = keys.shape[0]
    head_width = keys.shape[1]
    head_count = queries.shape[1] // head_width
    score_scale = head_width ** (-0.5)
    doc_span = 2 * row_count
    device_pos = lax.axis_index("ctx")
    block_index = jnp.arange(block_seq.shape[0], dtype=jnp.int32)
    own_block = jnp.sum(jnp.where(block_index == device_pos, block_seq, 0))
    kv_pair = jnp.concatenate([keys, values], axis=1)
    remote = [passed_along(kv_pair, "ctx", offset) for offset in (-1, 1, 2, 3)]
    candidates = jnp.stack([remote[0], kv_pair] + remote[1:])
    slot_total = 5
    row_offsets = jnp.arange(row_count, dtype=jnp.int32)
    slot_list = []
    block_parts = []
    position_parts = []
    for back_step in range(3):
        needed = own_block - back_step
        holder = jnp.sum(jnp.where(block_seq == needed, block_index, 0))
        slot = jnp.clip(device_pos - holder + 1, 0, 4)
        slot_list.append(slot)
        block_parts.append(lax.dynamic_index_in_dim(candidates, slot, 0, keepdims=False))
        position_parts.append(needed * row_count + row_offsets)
    fetched = jnp.concatenate(block_parts, axis=0)
    key_rows = fetched[:, :head_width]
    value_rows = fetched[:, head_width:]
    key_pos = jnp.concatenate(position_parts)
    query_pos = own_block * row_count + row_offsets
    lower_bound = jnp.clip(doc_start, jnp.maximum(query_pos - doc_span + 1, 0), query_pos)
    visible = (key_pos[None, :] <= query_pos[:, None]) & (key_pos[None, :] >= lower_bound[:, None])
    key_sum = jnp.zeros((3 * row_count, head_width), jnp.float32)
    value_sum = jnp.zeros((3 * row_count, head_width), jnp.float32)
    grad_heads_list = []
    for head_pos in range(head_count):
        query_head = queries[:, head_pos * head_width : (head_pos + 1) * head_width]
        grad_head = out_grad[:, head_pos * head_width : (head_pos + 1) * head_width]
        score = contract_rows(query_head, key_rows, 1, 1) * score_scale
        row_top = jnp.max(jnp.where(visible, score, -jnp.inf), axis=1, keepdims=True)
        weight = jnp.exp(jnp.where(visible, score - row_top, -jnp.inf))
        probability = weight / jnp.sum(weight, axis=1, keepdims=True)
        prob_grad = contract_rows(grad_head, value_rows, 1, 1)
        row_delta = jnp.sum(probability * prob_grad, axis=1, keepdims=True)
        score_grad = (probability * (prob_grad - row_delta)).astype(jnp.bfloat16)
        prob_round = probability.astype(jnp.bfloat16)
        grad_heads_list.append(
            jnp.dot(score_grad, key_rows, preferred_element_type=jnp.float32) * score_scale
        )
        key_sum = key_sum + contract_rows(score_grad, query_head, 0, 0)
        value_sum = value_sum + contract_rows(prob_round, grad_head, 0, 0)
    query_grad = jnp.concatenate(grad_heads_list, axis=1).astype(jnp.bfloat16)
    grads = jnp.concatenate([key_sum * score_scale, value_sum], axis=1)
    slot_ids = jnp.arange(slot_total, dtype=jnp.int32)
    partial_value = jnp.zeros((slot_total, row_count, 2 * head_width), jnp.float32)
    for back_step in range(3):
        selector = (slot_ids == slot_list[back_step]).astype(jnp.float32)
        partial_value = (
            partial_value
            + selector[:, None, None]
            * grads[back_step * row_count : (back_step + 1) * row_count][None]
        )
    returned = [
        passed_along(partial_value[offset + 1].astype(jnp.bfloat16), "ctx", -offset).astype(
            jnp.float32
        )
        for offset in (-1, 1, 2, 3)
    ]
    total = partial_value[1] + returned[0] + returned[1] + returned[2] + returned[3]
    mine = lax.psum_scatter(
        total.astype(jnp.bfloat16), "head", scatter_dimension=0, tiled=True
    ).astype(jnp.float32)
    key_grad = mine[:, :head_width].astype(jnp.bfloat16)
    value_grad = mine[:, head_width:].astype(jnp.bfloat16)
    return (query_grad, key_grad, value_grad)


def solution(mesh):
    return jax.shard_map(
        shards,
        mesh=mesh,
        in_specs=(
            P("ctx", "head"),
            P("ctx", None),
            P("ctx", None),
            P("ctx", "head"),
            P("ctx"),
            P(),
        ),
        out_specs=(P("ctx", "head"), P(("ctx", "head"), None), P(("ctx", "head"), None)),
        check_vma=False,
    )
```

profile of v0, /device:TPU:1, one launch (start us, length us, event | category | flops | bytes accessed | tf_op | source)
XLA Modules:
  0.0 126.3 jit_solution(6548446760126936780)
XLA Ops:
  7.2 0.0 copy-start.2
  7.2 0.0 reduce-scatter.2.cloned.1.call-start
  7.2 1.0 constant_dynamic-update-slice_fusion.1
  8.2 0.9 constant_dynamic-update-slice_fusion
  9.1 5.1 %collective-permute-start = (bf16[512,256]{1,0:T(8,128)(2,1)S(1)}, bf16[512,256]{1,0:T(8,128)(2,1)S(1)}, u32[]{:S(2)}, u32[]{:S(2)}) collective-permute-start(bf16[512,256]{1,0:T(8,128)(2,1)S(1)} %constant_dynamic-update-slice_fusion), channel_id=1, source_target_pairs={{4,0},{8,4},{12,8},{16,12},{20,16},{24,20},{28,24},{32,28},{36,32}... | collective-permute-start | bytes 786440 | tf_op jit(solution)/shard_map/ppermute | solution.py:10
  14.3 1.9 %collective-permute-start.1 = (bf16[512,256]{1,0:T(8,128)(2,1)S(1)}, bf16[512,256]{1,0:T(8,128)(2,1)S(1)}, u32[]{:S(2)}, u32[]{:S(2)}) collective-permute-start(bf16[512,256]{1,0:T(8,128)(2,1)S(1)} %constant_dynamic-update-slice_fusion), channel_id=1, source_target_pairs={{0,4},{4,8},{8,12},{12,16},{16,20},{20,24},{24,28},{28,32},{32,36}... | collective-permute-start | bytes 786440 | tf_op jit(solution)/shard_map/ppermute | solution.py:10
  16.2 3.3 %collective-permute-start.2 = (bf16[512,256]{1,0:T(8,128)(2,1)S(1)}, bf16[512,256]{1,0:T(8,128)(2,1)S(1)}, u32[]{:S(2)}, u32[]{:S(2)}) collective-permute-start(bf16[512,256]{1,0:T(8,128)(2,1)S(1)} %constant_dynamic-update-slice_fusion), channel_id=1, source_target_pairs={{0,8},{4,12},{8,16},{12,20},{16,24},{20,28},{24,32},{28,36},{32,40... | collective-permute-start | bytes 786440 | tf_op jit(solution)/shard_map/ppermute | solution.py:10
  19.6 4.0 %collective-permute-start.3 = (bf16[512,256]{1,0:T(8,128)(2,1)S(1)}, bf16[512,256]{1,0:T(8,128)(2,1)S(1)}, u32[]{:S(2)}, u32[]{:S(2)}) collective-permute-start(bf16[512,256]{1,0:T(8,128)(2,1)S(1)} %constant_dynamic-update-slice_fusion), channel_id=1, source_target_pairs={{0,12},{4,16},{8,20},{12,24},{16,28},{20,32},{24,36},{28,40},{32,4... | collective-permute-start | bytes 786440 | tf_op jit(solution)/shard_map/ppermute | solution.py:10
  23.6 1.3 %fusion.58 = s32[]{:T(128)} fusion(s32[64]{0:T(128)} %param.11, s32[]{:T(128)S(6)} %axis_index.15), kind=kLoop, calls=%fused_computation.128 | loop fusion | flops 191 | bytes 264 | tf_op jit(solution)/shard_map/reduce_sum | solution.py:30
  26.2 2.1 %fusion.59 = (s32[]{:T(128)}, s32[]{:T(128)}, s32[]{:T(128)}) fusion(s32[64]{0:T(128)} %param.11, s32[]{:T(128)} %fusion.58, s32[]{:T(128)S(6)} %sub.82, s32[]{:T(128)S(6)} %sub.81), kind=kLoop, calls=%fused_computation.129 | loop fusion | flops 573 | bytes 280 | tf_op jit(solution)/shard_map/reduce_sum | solution.py:41
  30.9 0.7 maximum_minimum_fusion
  31.7 0.0 collective-permute-done
  31.7 0.0 collective-permute-done.1
  31.8 0.0 collective-permute-done.2
  31.8 0.0 collective-permute-done.3
  31.8 0.1 dynamic-slice_bitcast_fusion.2
  31.9 0.1 pad_maximum_fusion
  32.0 0.0 copy-done.2
  32.0 0.6 fusion.1
  32.6 0.0 copy-start.4
  32.6 0.6 fusion.2
  33.2 0.6 fusion.3
  33.7 0.0 copy-done.4
  33.7 0.6 convolution_bitcast_fusion
  34.3 0.8 select_reduce_fusion.3
  35.1 1.3 %fusion.6 = f32[512]{0:T(512)S(1)} fusion(f32[512,1536]{0,1:T(8,128)S(1)} %get-tuple-element.37, f32[512]{0:T(512)S(1)} %get-tuple-element.36, s32[512]{0:T(512)S(1)} %get-tuple-element.41, s32[512]{0:T(512)S(1)} %get-tuple-element.42, s32[1536]{0:T(1024)S(1)} %pad_add_fusion), kind=kLoop, calls=%fused_computation.38 | loop fusion | flops 4718080 | bytes 3160064 | tf_op jit(solution)/shard_map/reduce_sum | solution.py:62
  36.4 1.2 fusion.16
  37.6 1.9 %multiply_reduce_fusion.3 = (f32[512]{0:T(512)S(1)}, f32[512]{0:T(512)S(1)}, f32[512]{0:T(512)S(1)}, f32[512]{0:T(512)S(1)}, f32[512,1536]{0,1:T(8,128)S(1)}) fusion(f32[512]{0:T(512)S(1)} %fusion.6, f32[512,1536]{0,1:T(8,128)S(1)} %get-tuple-element.37, f32[512]{0:T(512)S(1)} %get-tuple-element.36, s32[512]{0:T(512)S(1)} %get-tuple-element.41, ...), kind=kOutput, calls=%fused_computation.25 | convolution fusion | flops 212334592 | bytes 16277504 | tf_op jit(solution)/shard_map/dot_general | solution.py:14
  39.5 1.5 %fusion.8 = f32[512]{0:T(512)S(1)} fusion(f32[512,1536]{0,1:T(8,128)S(1)} %fusion.1, f32[512]{0:T(512)S(1)} %get-tuple-element.7, s32[512]{0:T(512)S(1)} %get-tuple-element.41, s32[512]{0:T(512)S(1)} %get-tuple-element.42, s32[1536]{0:T(1024)S(1)} %pad_add_fusion), kind=kLoop, calls=%fused_computation.40 | loop fusion | flops 4718080 | bytes 3160064 | tf_op jit(solution)/shard_map/reduce_sum | solution.py:62
  41.0 1.2 convolution_add_fusion.2
  42.2 3.3 %multiply_reduce_fusion.2 = (f32[512]{0:T(512)S(1)}, f32[512]{0:T(512)S(1)}, f32[512]{0:T(512)S(1)}, bf16[512,1536]{0,1:T(8,128)(2,1)S(1)}, f32[512,1536]{0,1:T(8,128)S(1)}) fusion(f32[512]{0:T(512)S(1)} %fusion.8, f32[512,1536]{0,1:T(8,128)S(1)} %fusion.1, f32[512]{0:T(512)S(1)} %get-tuple-element.7, s32[512]{0:T(512)S(1)} %get-tuple-element.41, ...), kind=kOutput, calls=%fused_computation.21 | convolution fusion | flops 217053696 | bytes 21004288 | tf_op jit(solution)/shard_map/dot_general | solution.py:14
  45.5 0.0 copy-start.3
  45.5 0.7 fusion.47
  46.2 1.2 convolution_add_fusion.1
  47.4 1.2 convolution_add_fusion
  48.6 2.9 %multiply_reduce_fusion.1 = (f32[512]{0:T(512)S(1)}, f32[512]{0:T(512)S(1)}, bf16[512,1536]{0,1:T(8,128)(2,1)S(1)}, f32[512,1536]{0,1:T(8,128)S(1)}) fusion(f32[512]{0:T(512)S(1)} %get-tuple-element.11, f32[512,1536]{0,1:T(8,128)S(1)} %fusion.2, f32[512]{0:T(512)S(1)} %get-tuple-element.8, s32[512]{0:T(512)S(1)} %get-tuple-element.41, ...), kind=kOutput, calls=%fused_computation.17 | convolution fusion | flops 216267776 | bytes 21002240 | tf_op jit(solution)/shard_map/dot_general | solution.py:14
  51.4 0.4 fusion.19
  51.9 0.6 convolution_add_fusion.5
  52.5 2.4 %multiply_convert_fusion.1 = (bf16[512,1536]{0,1:T(8,128)(2,1)S(1)}, bf16[512,1536]{0,1:T(8,128)(2,1)S(1)}) fusion(f32[512,1536]{0,1:T(8,128)S(1)} %get-tuple-element.40, f32[512]{0:T(512)S(1)} %get-tuple-element.13, f32[512]{0:T(512)S(1)} %get-tuple-element.11, f32[512,1536]{0,1:T(8,128)S(1)} %fusion.2, f32[512]{0:T(512)S(1)} %get-tuple-element.8, ...), kind=kLoop, calls=%fused_computation.16 | loop fusion | flops 11796480 | bytes 15751168 | tf_op jit(solution)/shard_map/convert_element_type | solution.py:65
  55.0 0.7 convolution_add_fusion.4
  55.7 0.7 fusion.4
  56.3 0.0 copy-done
  56.3 1.1 fusion.23
  57.4 0.2 copy.10
  57.6 1.2 copy.11
  58.9 2.0 %copy.9 = f32[512,256]{1,0:T(8,128)} copy(f32[512,256]{0,1:T(8,128)} %get-tuple-element.20) | data formatting | bytes 1048576 | tf_op jit(solution)/shard_map/slice | solution.py:81
  60.9 1.7 %fusion.62 = (bf16[5,512,256]{2,1,0:T(8,128)(2,1)S(1)}, f32[5,512,256]{2,1,0:T(8,128)S(1)}) fusion(f32[512,256]{1,0:T(8,128)S(1)} %copy.11, f32[5]{0:T(128)S(1)} %get-tuple-element.45, f32[512,256]{1,0:T(8,128)S(1)} %copy.10, f32[5]{0:T(128)S(1)} %get-tuple-element.46, f32[512,256]{1,0:T(8,128)} %copy.9, f32[5]{0:T(128)S(1)} %compare_convert_fusion.2), kind=kLoop, calls=%fused_computation.132 | loop fusion | flops 3932160 | bytes 5505084 | tf_op jit(solution)/shard_map/convert.5
  62.6 0.1 slice_bitcast_fusion.4
  62.7 5.7 %collective-permute-start.4 = (bf16[512,256]{1,0:T(8,128)(2,1)S(1)}, bf16[512,256]{1,0:T(8,128)(2,1)S(1)}, u32[]{:S(2)}, u32[]{:S(2)}) collective-permute-start(bf16[512,256]{1,0:T(8,128)(2,1)S(1)} %get-tuple-element.23), channel_id=1, source_target_pairs={{0,4},{4,8},{8,12},{12,16},{16,20},{20,24},{24,28},{28,32},{32,36}... | collective-permute-start | bytes 786440 | tf_op jit(solution)/shard_map/ppermute | solution.py:10
  68.4 1.9 %collective-permute-start.5 = (bf16[512,256]{1,0:T(8,128)(2,1)S(1)}, bf16[512,256]{1,0:T(8,128)(2,1)S(1)}, u32[]{:S(2)}, u32[]{:S(2)}) collective-permute-start(bf16[512,256]{1,0:T(8,128)(2,1)S(1)} %get-tuple-element.26), channel_id=1, source_target_pairs={{4,0},{8,4},{12,8},{16,12},{20,16},{24,20},{28,24},{32,28},{36,32}... | collective-permute-start | bytes 786440 | tf_op jit(solution)/shard_map/ppermute | solution.py:10
  70.3 1.3 %collective-permute-start.6 = (bf16[512,256]{1,0:T(8,128)(2,1)S(1)}, bf16[512,256]{1,0:T(8,128)(2,1)S(1)}, u32[]{:S(2)}, u32[]{:S(2)}) collective-permute-start(bf16[512,256]{1,0:T(8,128)(2,1)S(1)} %get-tuple-element.25), channel_id=1, source_target_pairs={{8,0},{12,4},{16,8},{20,12},{24,16},{28,20},{32,24},{36,28},{40,32... | collective-permute-start | bytes 786440 | tf_op jit(solution)/shard_map/ppermute | solution.py:10
  71.6 1.3 %collective-permute-start.7 = (bf16[512,256]{1,0:T(8,128)(2,1)S(1)}, bf16[512,256]{1,0:T(8,128)(2,1)S(1)}, u32[]{:S(2)}, u32[]{:S(2)}) collective-permute-start(bf16[512,256]{1,0:T(8,128)(2,1)S(1)} %get-tuple-element.24), channel_id=1, source_target_pairs={{12,0},{16,4},{20,8},{24,12},{28,16},{32,20},{36,24},{40,28},{44,3... | collective-permute-start | bytes 786440 | tf_op jit(solution)/shard_map/ppermute | solution.py:10
  72.9 0.4 fusion.20
  73.4 0.0 collective-permute-done.4
  73.4 4.1 %collective-permute-done.5 = bf16[512,256]{1,0:T(8,128)(2,1)S(1)} collective-permute-done((bf16[512,256]{1,0:T(8,128)(2,1)S(1)}, bf16[512,256]{1,0:T(8,128)(2,1)S(1)}, u32[]{:S(2)}, u32[]{:S(2)}) %collective-permute-start.5) | collective-permute-done | bytes 262176 | tf_op jit(solution)/shard_map/ppermute | solution.py:10
  77.5 3.1 %collective-permute-done.6 = bf16[512,256]{1,0:T(8,128)(2,1)S(1)} collective-permute-done((bf16[512,256]{1,0:T(8,128)(2,1)S(1)}, bf16[512,256]{1,0:T(8,128)(2,1)S(1)}, u32[]{:S(2)}, u32[]{:S(2)}) %collective-permute-start.6) | collective-permute-done | bytes 262176 | tf_op jit(solution)/shard_map/ppermute | solution.py:10
  80.6 8.7 %collective-permute-done.7 = bf16[512,256]{1,0:T(8,128)(2,1)S(1)} collective-permute-done((bf16[512,256]{1,0:T(8,128)(2,1)S(1)}, bf16[512,256]{1,0:T(8,128)(2,1)S(1)}, u32[]{:S(2)}, u32[]{:S(2)}) %collective-permute-start.7) | collective-permute-done | bytes 262176 | tf_op jit(solution)/shard_map/ppermute | solution.py:10
  89.2 0.9 fusion.28
  90.1 0.0 reduce-scatter.2.cloned.1.call-update
  90.2 0.4 fusion.21
  90.6 1.8 %fusion.18 = bf16[512,128]{0,1:T(8,128)(2,1)S(1)} fusion(bf16[512,1536]{0,1:T(8,128)(2,1)} %copy-done.3, bf16[1536,256]{1,0:T(8,128)(2,1)S(1)} %pad_maximum_fusion), kind=kOutput, calls=%fused_computation.58 | convolution fusion | flops 201457664 | bytes 2097152 | tf_op jit(solution)/shard_map/dot_general | solution.py:68
  92.5 1.0 copy.12
  93.5 24.6 %reduce-scatter.2.cloned.1.call-done = bf16[128,256]{1,0:T(8,128)(2,1)} async-done(((bf16[512,256]{1,0:T(8,128)(2,1)}), bf16[128,256]{1,0:T(8,128)(2,1)}) %reduce-scatter.2.cloned.1.call-update) | async-done | bytes 65552 | tf_op jit(solution)/shard_map/reduce_scatter | solution.py:90
  118.1 1.4 %fusion.67 = (bf16[128,128]{1,0:T(8,128)(2,1)}, bf16[128,128]{1,0:T(8,128)(2,1)}) fusion(bf16[128,256]{1,0:T(8,128)(2,1)} %reduce-scatter.2.cloned.1.call-done), kind=kLoop, calls=%fused_computation.133 | loop fusion | bytes 131072 | tf_op jit(solution)/shard_map/slice | solution.py:94
  (14 shorter events, 0.2 us)
Async XLA Ops:
  7.2 24.8 %copy-start.2 = (bf16[512,512]{1,0:T(8,128)(2,1)S(1)}, bf16[512,512]{1,0:T(8,128)(2,1)}, u32[]{:S(2)}) copy-start(bf16[512,512]{1,0:T(8,128)(2,1)} %param.6) | copy-start | bytes 1572868
  7.2 110.9 %reduce-scatter.2.cloned.1.call-start = ((), (), s32[]{:S(2)}) async-start(), calls=%async_computation.1 | async-start | bytes 327680 | tf_op jit(solution)/shard_map/reduce_scatter | solution.py:90
  9.1 22.5 %collective-permute-start = (bf16[512,256]{1,0:T(8,128)(2,1)S(1)}, bf16[512,256]{1,0:T(8,128)(2,1)S(1)}, u32[]{:S(2)}, u32[]{:S(2)}) collective-permute-start(bf16[512,256]{1,0:T(8,128)(2,1)S(1)} %constant_dynamic-update-slice_fusion), channel_id=1, source_target_pairs={{4,0},{8,4},{12,8},{16,12},{20,16},{24,20},{28,24},{32,28},{36,32}... | collective-permute-start | bytes 786440 | tf_op jit(solution)/shard_map/ppermute | solution.py:10
  14.3 17.4 %collective-permute-start.1 = (bf16[512,256]{1,0:T(8,128)(2,1)S(1)}, bf16[512,256]{1,0:T(8,128)(2,1)S(1)}, u32[]{:S(2)}, u32[]{:S(2)}) collective-permute-start(bf16[512,256]{1,0:T(8,128)(2,1)S(1)} %constant_dynamic-update-slice_fusion), channel_id=1, source_target_pairs={{0,4},{4,8},{8,12},{12,16},{16,20},{20,24},{24,28},{28,32},{32,36}... | collective-permute-start | bytes 786440 | tf_op jit(solution)/shard_map/ppermute | solution.py:10
  16.2 15.5 %collective-permute-start.2 = (bf16[512,256]{1,0:T(8,128)(2,1)S(1)}, bf16[512,256]{1,0:T(8,128)(2,1)S(1)}, u32[]{:S(2)}, u32[]{:S(2)}) collective-permute-start(bf16[512,256]{1,0:T(8,128)(2,1)S(1)} %constant_dynamic-update-slice_fusion), channel_id=1, source_target_pairs={{0,8},{4,12},{8,16},{12,20},{16,24},{20,28},{24,32},{28,36},{32,40... | collective-permute-start | bytes 786440 | tf_op jit(solution)/shard_map/ppermute | solution.py:10
  19.6 12.2 %collective-permute-start.3 = (bf16[512,256]{1,0:T(8,128)(2,1)S(1)}, bf16[512,256]{1,0:T(8,128)(2,1)S(1)}, u32[]{:S(2)}, u32[]{:S(2)}) collective-permute-start(bf16[512,256]{1,0:T(8,128)(2,1)S(1)} %constant_dynamic-update-slice_fusion), channel_id=1, source_target_pairs={{0,12},{4,16},{8,20},{12,24},{16,28},{20,32},{24,36},{28,40},{32,4... | collective-permute-start | bytes 786440 | tf_op jit(solution)/shard_map/ppermute | solution.py:10
  32.6 1.2 copy-start.4
  45.5 1.8 %copy-start.3 = (bf16[512,1536]{0,1:T(8,128)(2,1)}, bf16[512,1536]{0,1:T(8,128)(2,1)S(1)}, u32[]{:S(2)}) copy-start(bf16[512,1536]{0,1:T(8,128)(2,1)S(1)} %get-tuple-element.32) | copy-start | bytes 4718596
  55.0 1.3 %copy-start = (bf16[512,1536]{0,1:T(8,128)(2,1)}, bf16[512,1536]{0,1:T(8,128)(2,1)S(1)}, u32[]{:S(2)}) copy-start(bf16[512,1536]{0,1:T(8,128)(2,1)S(1)} %get-tuple-element.34) | copy-start | bytes 4718596
  60.9 12.0 %copy-start.1 = (bf16[512,1536]{0,1:T(8,128)(2,1)S(1)}, bf16[512,1536]{0,1:T(8,128)(2,1)}, u32[]{:S(2)}) copy-start(bf16[512,1536]{0,1:T(8,128)(2,1)} %copy-done) | copy-start | bytes 4718596
  62.7 10.7 %collective-permute-start.4 = (bf16[512,256]{1,0:T(8,128)(2,1)S(1)}, bf16[512,256]{1,0:T(8,128)(2,1)S(1)}, u32[]{:S(2)}, u32[]{:S(2)}) collective-permute-start(bf16[512,256]{1,0:T(8,128)(2,1)S(1)} %get-tuple-element.23), channel_id=1, source_target_pairs={{0,4},{4,8},{8,12},{12,16},{16,20},{20,24},{24,28},{28,32},{32,36}... | collective-permute-start | bytes 786440 | tf_op jit(solution)/shard_map/ppermute | solution.py:10
  68.4 9.1 %collective-permute-start.5 = (bf16[512,256]{1,0:T(8,128)(2,1)S(1)}, bf16[512,256]{1,0:T(8,128)(2,1)S(1)}, u32[]{:S(2)}, u32[]{:S(2)}) collective-permute-start(bf16[512,256]{1,0:T(8,128)(2,1)S(1)} %get-tuple-element.26), channel_id=1, source_target_pairs={{4,0},{8,4},{12,8},{16,12},{20,16},{24,20},{28,24},{32,28},{36,32}... | collective-permute-start | bytes 786440 | tf_op jit(solution)/shard_map/ppermute | solution.py:10
  70.3 10.3 %collective-permute-start.6 = (bf16[512,256]{1,0:T(8,128)(2,1)S(1)}, bf16[512,256]{1,0:T(8,128)(2,1)S(1)}, u32[]{:S(2)}, u32[]{:S(2)}) collective-permute-start(bf16[512,256]{1,0:T(8,128)(2,1)S(1)} %get-tuple-element.25), channel_id=1, source_target_pairs={{8,0},{12,4},{16,8},{20,12},{24,16},{28,20},{32,24},{36,28},{40,32... | collective-permute-start | bytes 786440 | tf_op jit(solution)/shard_map/ppermute | solution.py:10
  71.6 17.6 %collective-permute-start.7 = (bf16[512,256]{1,0:T(8,128)(2,1)S(1)}, bf16[512,256]{1,0:T(8,128)(2,1)S(1)}, u32[]{:S(2)}, u32[]{:S(2)}) collective-permute-start(bf16[512,256]{1,0:T(8,128)(2,1)S(1)} %get-tuple-element.24), channel_id=1, source_target_pairs={{12,0},{16,4},{20,8},{24,12},{28,16},{32,20},{36,24},{40,28},{44,3... | collective-permute-start | bytes 786440 | tf_op jit(solution)/shard_map/ppermute | solution.py:10
Sparse Core Ops, SparseCore 0:
  90.3 27.7 reduce-scatter.1
where the time goes:
time: 128 us; the launch traced here: 126 us
  waiting for transfers between devices  40.5 us (32%)
  starting transfers between devices  24.7 us (19%)
  matrix products  21.7 us (17%)
  between operations  18.4 us (14%)
  other arithmetic  13 us (10%)
  local copies, waits for them, and re-layouts  8.04 us (6%)
    ppermute x8, starting transfers between devices, passed_along(): return lax.ppermute(block, axis, route)  24.6 us
    reduce_scatter x1, waiting for transfers between devices, shards(): lax.psum_scatter(total.astype(jnp.bfloat16), 'head', scatter_dimension=0,...  24.6 us
    dot_general x16, matrix products, contract_rows(): lax.dot_general(left_side, right_side, (((left_axis,), (right_axis,)), ((...  18.6 us
    ppermute x8, waiting for transfers between devices, passed_along(): return lax.ppermute(block, axis, route)  15.9 us
    slice x3, local copies, waits for them, and re-layouts, shards(): grads[back_step * row_count:(back_step + 1) * row_count][None]  3.47 us
    dot_general x4, matrix products, shards(): jnp.dot(score_grad, key_rows, preferred_element_type=jnp.float32)  3.08 us
    reduce_sum x2, other arithmetic, shards(): probability = weight / jnp.sum(weight, axis=1, keepdims=True)  2.73 us
  transfers between devices with their start and end apart: 9, of which 4 were waited for; matrix products, arithmetic and copies ran while one was open for 6% of the time, Pallas kernels for 0%

commit v1 on v0

v1 whole, which is shorter than its diff:
```python
import functools
import math

import jax
import jax.numpy as jnp
from jax import lax
from jax.experimental import pallas as pl
from jax.experimental.pallas import tpu as pltpu
from jax.sharding import PartitionSpec as P

MESH = pl.DeviceIdType.MESH
ROWS = 512
WIDTH = 128
HEADS = 4
QT = 128
KT = 256
COLS = HEADS * QT
MASKED = -1e30
VMEM_LIMIT = 56 * 1024 * 1024


def copy_to(src, dst, send, recv, ctx, head):
    return pltpu.make_async_remote_copy(
        src_ref=src,
        dst_ref=dst,
        send_sem=send,
        recv_sem=recv,
        device_id=(ctx, head),
        device_id_type=MESH,
    )


def greet(senders, count):
    barrier = pltpu.get_barrier_semaphore()
    for ctx, head in senders:
        pl.semaphore_signal(barrier, inc=1, device_id=(ctx, head), device_id_type=MESH)
    pl.semaphore_wait(barrier, count)


def fetch_kernel(n_ctx, k_ref, v_ref, kv_ref, send_z, recv_z, send_f, recv_f, send_p, recv_p, local):
    me = lax.axis_index("ctx")
    head = lax.axis_index("head")
    core = lax.rem(me, 2)
    partner = me + 1 - 2 * core
    after = lax.rem(me + 2, n_ctx)
    before = lax.rem(me + n_ctx - 2, n_ctx)
    greet([(partner, head), (before, head), (after, head)], 3)
    half = ROWS // 2
    parts = [(j, r) for r in range(2) for j in range(2)]
    refs = (k_ref, v_ref)
    out = []
    for i, (j, r) in enumerate(parts):
        rows = pl.ds(r * half, half)
        cp = copy_to(refs[j].at[rows], kv_ref.at[2 + core, j, rows], send_z.at[i], recv_z.at[i], after, head)
        cp.start()
        out.append(cp)
    near = []
    own = []
    for j in range(2):
        cp = copy_to(refs[j], kv_ref.at[1, j], send_p.at[j], recv_p.at[j], partner, head)
        cp.start()
        near.append(cp)
        cp = pltpu.make_async_copy(refs[j], kv_ref.at[0, j], local.at[j])
        cp.start()
        own.append(cp)
    forwards = []
    for i, (j, r) in enumerate(parts):
        rows = pl.ds(r * half, half)
        out[i].wait_recv()
        cp = copy_to(
            kv_ref.at[2 + core, j, rows], kv_ref.at[2 + core, j, rows], send_f.at[i], recv_f.at[i], partner, head
        )
        cp.start()
        forwards.append(cp)
    for cp in own + near + forwards:
        cp.wait()
    for cp in out:
        cp.wait_send()


def fetch(keys, values, n_ctx):
    return pl.pallas_call(
        functools.partial(fetch_kernel, n_ctx),
        out_shape=jax.ShapeDtypeStruct((4, 2, ROWS, WIDTH), jnp.bfloat16),
        in_specs=[pl.BlockSpec(memory_space=pl.ANY)] * 2,
        out_specs=pl.BlockSpec(memory_space=pl.ANY),
        scratch_shapes=[pltpu.SemaphoreType.DMA((4,))] * 4 + [pltpu.SemaphoreType.DMA((2,))] * 3,
        compiler_params=pltpu.CompilerParams(collective_id=0, has_side_effects=True),
        name="fetch",
    )(keys, values)


def dot(a, b, ca, cb):
    return lax.dot_general(a, b, (((ca,), (cb,)), ((), ())), preferred_element_type=jnp.float32)


def attend_kernel(
    n_ctx,
    pos_ref,
    seq_ref,
    start_ref,
    lower_ref,
    q_ref,
    do_ref,
    kv_ref,
    dq_ref,
    own_ref,
    near_ref,
    prev_ref,
    acc,
    p_scr,
    dp_scr,
    m_scr,
):
    me = pos_ref[0]
    tile = pl.program_id(0)
    core = lax.rem(me, 2)
    chip_before = lax.rem(me - core + n_ctx - 2, n_ctx)
    own = seq_ref[me]
    odd = lax.rem(own, 2) == 1
    slot1 = jnp.where(odd, 1, jnp.where(seq_ref[chip_before] == own - 1, 2, 3))
    slot2 = jnp.where(seq_ref[chip_before] == own - 2, 2, 3)
    base = (own - 2) * ROWS
    scale = WIDTH ** (-0.5)
    scale2 = scale * math.log2(math.e)

    @pl.when(tile == 0)
    def _():
        acc[...] = jnp.zeros_like(acc)

    first_row = 2 * ROWS + tile * QT
    row_pos = first_row + lax.broadcasted_iota(jnp.int32, (1, QT), 1)
    lower = jnp.clip(lower_ref[pl.ds(tile, 1), :] - base, jnp.maximum(row_pos - 2 * ROWS + 1, -base), row_pos)
    lo = jnp.clip(start_ref[tile * QT] - base, jnp.maximum(first_row - 2 * ROWS + 1, -base), first_row)
    lo_tile = lo // KT
    hi_tile = (first_row + QT - 1) // KT + 1

    q = jnp.concatenate([q_ref[:, h * WIDTH : (h + 1) * WIDTH] for h in range(HEADS)], axis=0)
    do = jnp.concatenate([do_ref[:, h * WIDTH : (h + 1) * WIDTH] for h in range(HEADS)], axis=0)

    def kv_tile(kt, which):
        role = kt // 2
        slot = jnp.where(role == 2, 0, jnp.where(role == 1, slot1, slot2))
        return kv_ref[slot, which, pl.ds((kt % 2) * KT, KT), :]

    def first_pass(kt, carry):
        m, l, d = carry
        k = kv_tile(kt, 0)
        v = kv_tile(kt, 1)
        key_pos = kt * KT + lax.broadcasted_iota(jnp.int32, (KT, QT), 0)
        bias = jnp.where((key_pos >= lower) & (key_pos <= row_pos), 0.0, MASKED)
        s = dot(k, q, 1, 1)
        dp = dot(v, do, 1, 1)
        s = s * scale2 + jnp.concatenate([bias] * HEADS, axis=1)
        m_new = jnp.maximum(m, jnp.max(s, axis=0, keepdims=True))
        p = jnp.exp2(s - m_new)
        shrink = jnp.exp2(m - m_new)
        l = l * shrink + jnp.sum(p, axis=0, keepdims=True)
        d = d * shrink + jnp.sum(p * dp, axis=0, keepdims=True)
        p_scr[kt] = p
        dp_scr[kt] = dp
        m_scr[kt] = m_new
        return m_new, l, d

    zero = jnp.zeros((1, COLS), jnp.float32)
    m, l, d = lax.fori_loop(lo_tile, hi_tile, first_pass, (zero + MASKED, zero, zero))
    inv = 1.0 / l
    delta = d * inv

    def second_pass(kt, dq):
        k = kv_tile(kt, 0)
        factor = jnp.exp2(m_scr[kt] - m) * inv
        p = p_scr[kt] * factor
        ds = (p * (dp_scr[kt] - delta)).astype(jnp.bfloat16)
        pb = p.astype(jnp.bfloat16)
        rows = pl.ds(kt * KT, KT)
        acc[rows, 0:WIDTH] += dot(ds, q, 1, 0)
        acc[rows, WIDTH : 2 * WIDTH] += dot(pb, do, 1, 0)
        return dq + dot(k, ds, 0, 0)

    dq = lax.fori_loop(lo_tile, hi_tile, second_pass, jnp.zeros((WIDTH, COLS), jnp.float32))
    for h in range(HEADS):
        piece = dq[:, h * QT : (h + 1) * QT] * scale
        dq_ref[:, h * WIDTH : (h + 1) * WIDTH] = piece.T.astype(dq_ref.dtype)

    @pl.when(tile == pl.num_programs(0) - 1)
    def _():
        def grads(role):
            g = acc[role * ROWS : (role + 1) * ROWS, :]
            return jnp.concatenate([g[:, :WIDTH] * scale, g[:, WIDTH:]], axis=1)

        own_ref[...] = grads(2)
        g1 = grads(1).astype(jnp.bfloat16)
        g2 = grads(0).astype(jnp.bfloat16)
        none = jnp.zeros_like(g1)
        near_ref[...] = jnp.where(odd, g1, none)
        prev_ref[0] = jnp.where(slot1 == 2, g1, jnp.where(slot2 == 2, g2, none))
        prev_ref[1] = jnp.where(slot1 == 3, g1, jnp.where(slot2 == 3, g2, none))


def attend(queries, out_grad, doc_start, block_seq, kv, n_ctx, pos):
    steps = ROWS // QT
    smem = pl.BlockSpec(memory_space=pltpu.SMEM)
    whole = lambda shape: pl.BlockSpec(shape, lambda i: (0,) * len(shape))
    return pl.pallas_call(
        functools.partial(attend_kernel, n_ctx),
        grid=(steps,),
        out_shape=(
            jax.ShapeDtypeStruct(queries.shape, jnp.bfloat16),
            jax.ShapeDtypeStruct((ROWS, 2 * WIDTH), jnp.float32),
            jax.ShapeDtypeStruct((ROWS, 2 * WIDTH), jnp.bfloat16),
            jax.ShapeDtypeStruct((2, ROWS, 2 * WIDTH), jnp.bfloat16),
        ),
        in_specs=[
            smem,
            smem,
            smem,
            whole((steps, QT)),
            pl.BlockSpec((QT, HEADS * WIDTH), lambda i: (i, 0)),
            pl.BlockSpec((QT, HEADS * WIDTH), lambda i: (i, 0)),
            whole((4, 2, ROWS, WIDTH)),
        ],
        out_specs=(
            pl.BlockSpec((QT, HEADS * WIDTH), lambda i: (i, 0)),
            whole((ROWS, 2 * WIDTH)),
            whole((ROWS, 2 * WIDTH)),
            whole((2, ROWS, 2 * WIDTH)),
        ),
        scratch_shapes=[
            pltpu.VMEM((3 * ROWS, 2 * WIDTH), jnp.float32),
            pltpu.VMEM((3 * ROWS // KT, KT, COLS), jnp.float32),
            pltpu.VMEM((3 * ROWS // KT, KT, COLS), jnp.float32),
            pltpu.VMEM((3 * ROWS // KT, 1, COLS), jnp.float32),
        ],
        compiler_params=pltpu.CompilerParams(vmem_limit_bytes=VMEM_LIMIT),
        name="attend",
    )(pos, block_seq, doc_start, doc_start.reshape(steps, QT), queries, out_grad, kv)


def give_back_kernel(
    n_ctx,
    n_head,
    own_ref,
    near_ref,
    prev_ref,
    dk_ref,
    dv_ref,
    got_near,
    got_prev,
    own_sum,
    own_cast,
    prev_sum,
    got_x,
    got_z,
    send_p,
    recv_p,
    send_x,
    recv_x,
    send_z,
    recv_z,
):
    me = lax.axis_index("ctx")
    head = lax.axis_index("head")
    core = lax.rem(me, 2)
    partner = me + 1 - 2 * core
    after = lax.rem(me + 2, n_ctx)
    before = lax.rem(me + n_ctx - 2, n_ctx)
    others = [lax.rem(head + s, n_head) for s in range(1, n_head)]
    peers = [(partner, head)] + [(me, x) for x in others] + [(after, x) for x in [head] + others]
    greet(peers, len(peers))
    part = ROWS // n_head
    to_prev = copy_to(prev_ref.at[1 - core], got_prev, send_p.at[0], recv_p.at[0], partner, head)
    to_near = copy_to(near_ref, got_near, send_p.at[1], recv_p.at[1], partner, head)
    to_prev.start()
    to_near.start()
    copies = []
    to_prev.wait_recv()
    prev_sum[...] = (prev_ref[core].astype(jnp.float32) + got_prev[...].astype(jnp.float32)).astype(jnp.bfloat16)
    for s in range(n_head):
        x = lax.rem(head + s, n_head)
        cp = copy_to(prev_sum.at[pl.ds(x * part, part)], got_z.at[s], send_z.at[s], recv_z.at[s], before, x)
        cp.start()
        copies.append(cp)
    to_near.wait_recv()
    own_sum[...] = own_ref[...] + got_near[...].astype(jnp.float32)
    mine = own_sum[pl.ds(head * part, part), :]
    own_cast[...] = own_sum[...].astype(jnp.bfloat16)
    for s in range(1, n_head):
        x = lax.rem(head + s, n_head)
        cp = copy_to(own_cast.at[pl.ds(x * part, part)], got_x.at[s - 1], send_x.at[s - 1], recv_x.at[s - 1], me, x)
        cp.start()
        copies.append(cp)
    for cp in copies:
        cp.wait_recv()
    total = mine
    for s in range(n_head - 1):
        total = total + got_x[s].astype(jnp.float32)
    for s in range(n_head):
        total = total + got_z[s].astype(jnp.float32)
    dk_ref[...] = total[:, :WIDTH].astype(jnp.bfloat16)
    dv_ref[...] = total[:, WIDTH:].astype(jnp.bfloat16)
    for cp in [to_prev, to_near] + copies:
        cp.wait_send()


def give_back(own, near, prev, n_ctx, n_head):
    part = ROWS // n_head
    vmem = pl.BlockSpec(memory_space=pltpu.VMEM)
    bf16 = jnp.bfloat16
    return pl.pallas_call(
        functools.partial(give_back_kernel, n_ctx, n_head),
        out_shape=(jax.ShapeDtypeStruct((part, WIDTH), bf16),) * 2,
        in_specs=[vmem] * 3,
        out_specs=(vmem, vmem),
        scratch_shapes=[
            pltpu.VMEM((ROWS, 2 * WIDTH), bf16),
            pltpu.VMEM((ROWS, 2 * WIDTH), bf16),
            pltpu.VMEM((ROWS, 2 * WIDTH), jnp.float32),
            pltpu.VMEM((ROWS, 2 * WIDTH), bf16),
            pltpu.VMEM((ROWS, 2 * WIDTH), bf16),
            pltpu.VMEM((n_head - 1, part, 2 * WIDTH), bf16),
            pltpu.VMEM((n_head, part, 2 * WIDTH), bf16),
            pltpu.SemaphoreType.DMA((2,)),
            pltpu.SemaphoreType.DMA((2,)),
            pltpu.SemaphoreType.DMA((n_head - 1,)),
            pltpu.SemaphoreType.DMA((n_head - 1,)),
            pltpu.SemaphoreType.DMA((n_head,)),
            pltpu.SemaphoreType.DMA((n_head,)),
        ],
        compiler_params=pltpu.CompilerParams(
            collective_id=1, has_side_effects=True, vmem_limit_bytes=VMEM_LIMIT
        ),
        name="give_back",
    )(own, near, prev)


def shards(queries, keys, values, out_grad, doc_start, block_seq):
    n_ctx = lax.axis_size("ctx")
    n_head = lax.axis_size("head")
    pos = lax.axis_index("ctx").astype(jnp.int32).reshape(1)
    kv = fetch(keys, values, n_ctx)
    query_grad, own, near, prev = attend(queries, out_grad, doc_start, block_seq, kv, n_ctx, pos)
    key_grad, value_grad = give_back(own, near, prev, n_ctx, n_head)
    return query_grad, key_grad, value_grad


def solution(mesh):
    return jax.shard_map(
        shards,
        mesh=mesh,
        in_specs=(
            P("ctx", "head"),
            P("ctx", None),
            P("ctx", None),
            P("ctx", "head"),
            P("ctx"),
            P(),
        ),
        out_specs=(P("ctx", "head"), P(("ctx", "head"), None), P(("ctx", "head"), None)),
        check_vma=False,
    )
```

time: 128 us -> 47 us (0.37); the launches traced: 126 us -> 46.8 us
  Pallas kernels: 0 us -> 44.1 us
  waiting for transfers between devices: 40.5 us -> 0 us
  starting transfers between devices: 24.7 us -> 0 us
  matrix products: 21.7 us -> 0 us
  between operations: 18.4 us -> 0.66 us
  other arithmetic: 13 us -> 0 us
  local copies, waits for them, and re-layouts: 8.04 us -> 2 us
    pallas_call x0 -> x3, Pallas kernels: none -> 44.1 us  [the longest x1 18.6 us: fetch(): pl.pallas_call(functools.partial(fetch_kernel, n_ctx), out_shape=jax.Shap...]
    ppermute x8 -> x0, starting transfers between devices: 24.6 us -> none  [passed_along(): return lax.ppermute(block, axis, route)]
    reduce_scatter x1 -> x0, waiting for transfers between devices: 24.6 us -> none  [shards(): lax.psum_scatter(total.astype(jnp.bfloat16), 'head', scatter_dimension=0,...]
    dot_general x20 -> x0, matrix products: 21.7 us -> none  [the longest x16 18.6 us: contract_rows(): lax.dot_general(left_side, right_side, (((left_axis,), (right_axis,)), ((...]
    ppermute x8 -> x0, waiting for transfers between devices: 15.9 us -> none  [passed_along(): return lax.ppermute(block, axis, route)]
    reduce_sum x4 -> x0, other arithmetic: 6.08 us -> none  [the longest x2 2.73 us: shards(): probability = weight / jnp.sum(weight, axis=1, keepdims=True)]
    slice x4 -> x0, local copies, waits for them, and re-layouts: 4.87 us -> none  [the longest x3 3.47 us: shards(): grads[back_step * row_count:(back_step + 1) * row_count][None]]
    convert_element_type x4 -> x0, other arithmetic: 3.34 us -> none  [the longest x1 2.45 us: shards(): score_grad = (probability * (prob_grad - row_delta)).astype(jnp.bfloat16)]
  transfers between devices with their start and end apart: 9 -> 0, of which waited for: 4 -> 0; matrix products, arithmetic and copies ran while one was open for 6% -> 0% of each run, Pallas kernels for 0% -> 0%
where the time goes in v1:
time: 47 us; the launch traced here: 46.8 us
  Pallas kernels  44.1 us (94%)
  local copies, waits for them, and re-layouts  2 us (4%)
  between operations  0.66 us (1%)
    pallas_call x1, Pallas kernels, fetch(): pl.pallas_call(functools.partial(fetch_kernel, n_ctx), out_shape=jax.Shap...  18.6 us
    pallas_call x1, Pallas kernels, give_back(): pl.pallas_call(functools.partial(give_back_kernel, n_ctx, n_head), out_sh...  14.9 us
    pallas_call x1, Pallas kernels, attend(): pl.pallas_call(functools.partial(attend_kernel, n_ctx), grid=(steps,), ou...  10.6 us
    unnamed x4, local copies, waits for them, and re-layouts  2 us

profile of v1, /device:TPU:1, one launch (start us, length us, event | category | flops | bytes accessed | tf_op | source)
XLA Modules:
  0.0 46.8 jit_solution(2769704806266698136)
XLA Ops:
  0.6 18.6 %fetch.1.kv_ref = bf16[4,2,512,128]{3,2,1,0:T(8,128)(2,1)} custom-call(bf16[512,128]{1,0:T(8,128)(2,1)} %k_ref.1, bf16[512,128]{1,0:T(8,128)(2,1)} %v_ref.1), custom_call_target="tpu_custom_call" | custom-call | tf_op jit(solution)/shard_map/fetch/pallas_call | solution.py:82
  19.3 10.6 %attend.1 = (bf16[512,512]{1,0:T(8,128)(2,1)}, f32[512,256]{1,0:T(8,128)}, bf16[512,256]{1,0:T(8,128)(2,1)}, bf16[2,512,256]{2,1,0:T(8,128)(2,1)}) custom-call(s32[1]{0:T(128)} %bitcast.pos_ref, s32[64]{0:T(128)} %seq_ref.1, s32[512]{0:T(512)} %start_ref.1, s32[4,128]{1,0:T(4,128)} %bitcast.2, bf16[512,512]{1,0:T(8,128)(2,1)} %q_ref.1, ...), custom_call_target="tpu_custom_call" | custom-call | tf_op jit(solution)/shard_map/attend/pallas_call | solution.py:205
  29.9 14.9 %give_back.1 = (bf16[128,128]{1,0:T(8,128)(2,1)}, bf16[128,128]{1,0:T(8,128)(2,1)}) custom-call(f32[512,256]{1,0:T(8,128)} %get-tuple-element.10.own_ref, bf16[512,256]{1,0:T(8,128)(2,1)} %get-tuple-element.11.near_ref, bf16[2,512,256]{2,1,0:T(8,128)(2,1)} %get-tuple-element.12.prev_ref), custom_call_target="tpu_custom_call" | custom-call | tf_op jit(solution)/shard_map/give_back/pallas_call | solution.py:310
  44.8 0.0 copy-start
  44.8 1.4 %copy.11 = bf16[128,128]{1,0:T(8,128)(2,1)} copy(bf16[128,128]{1,0:T(8,128)(2,1)} %get-tuple-element.19) | data formatting | bytes 65536
  46.1 0.0 copy-done
  46.2 0.6 %copy.12 = bf16[128,128]{1,0:T(8,128)(2,1)} copy(bf16[128,128]{1,0:T(8,128)(2,1)S(1)} %copy-done) | data formatting | bytes 65536
Async XLA Ops:
  44.8 1.4 %copy-start = (bf16[128,128]{1,0:T(8,128)(2,1)S(1)}, bf16[128,128]{1,0:T(8,128)(2,1)}, u32[]{:S(2)}) copy-start(bf16[128,128]{1,0:T(8,128)(2,1)} %get-tuple-element.20) | copy-start | bytes 98308

commit v2 on v0

v2 whole, which is shorter than its diff:
```python
import functools
import math

import jax
import jax.numpy as jnp
from jax import lax
from jax.experimental import pallas as pl
from jax.experimental.pallas import tpu as pltpu
from jax.sharding import PartitionSpec as P

MESH = pl.DeviceIdType.MESH

ROWS = 512
WIDTH = 128
HEADS = 4
QT = 128
TILES = ROWS // QT
COLS = HEADS * QT
MASKED = -1e30
HALVES = 2
HALF = ROWS // HALVES
VMEM_LIMIT = 60 * 1024 * 1024
SCALE = WIDTH ** (-0.5)
SCALE2 = SCALE * math.log2(math.e)


def dot(a, b, ca, cb):
    return lax.dot_general(a, b, (((ca,), (cb,)), ((), ())), preferred_element_type=jnp.float32)


def bias_of(lower_ref, base, t, role, first_key, n_keys):
    row_pos = 2 * ROWS + t * QT + lax.broadcasted_iota(jnp.int32, (1, QT), 1)
    lower = jnp.clip(lower_ref[pl.ds(t, 1), :] - base, jnp.maximum(row_pos - 2 * ROWS + 1, -base), row_pos)
    key_pos = (2 - role) * ROWS + first_key + lax.broadcasted_iota(jnp.int32, (n_keys, QT), 0)
    seen = key_pos >= lower
    if role == 0:
        seen = seen & (key_pos <= row_pos)
    return jnp.where(seen, 0.0, MASKED)


def pass_one(role, t, first_key, n_keys, k, v, q, do, lower_ref, base, p_scr, dp_scr, m_scr, l_scr, d_scr):
    bias = bias_of(lower_ref, base, t, role, first_key, n_keys)
    s = dot(k, q, 1, 1) * SCALE2 + jnp.concatenate([bias] * HEADS, axis=1)
    dp = dot(v, do, 1, 1)
    top = jnp.max(s, axis=0, keepdims=True)
    if role > 0:
        m_old = m_scr[role - 1, t]
        m = jnp.maximum(m_old, top)
        shrink = jnp.exp2(m_old - m)
    else:
        m = top
    p = jnp.exp2(s - m)
    l = jnp.sum(p, axis=0, keepdims=True)
    d = jnp.sum(p * dp, axis=0, keepdims=True)
    if role > 0:
        l = l + l_scr[t] * shrink
        d = d + d_scr[t] * shrink
    m_scr[role, t] = m
    l_scr[t] = l
    d_scr[t] = d
    rows = pl.ds(first_key, n_keys)
    p_scr[role, t, rows, :] = p
    dp_scr[role, t, rows, :] = dp


def pass_two(role, t, first_key, n_keys, k, q, do, p_scr, dp_scr, m_scr, l_scr, d_scr, dq_acc):
    inv = 1.0 / l_scr[t]
    delta = d_scr[t] * inv
    factor = jnp.exp2(m_scr[role, t] - m_scr[2, t]) * inv
    rows = pl.ds(first_key, n_keys)
    p = p_scr[role, t, rows, :] * factor
    ds = (p * (dp_scr[role, t, rows, :] - delta)).astype(jnp.bfloat16)
    pb = p.astype(jnp.bfloat16)
    dq = dot(k, ds, 0, 0)
    if role == 1:
        dq_acc[t] = dq
    else:
        dq_acc[t] += dq
    return dot(ds, q, 1, 0), dot(pb, do, 1, 0)


def copy_to(src, dst, send, recv, ctx, head):
    return pltpu.make_async_remote_copy(
        src_ref=src,
        dst_ref=dst,
        send_sem=send,
        recv_sem=recv,
        device_id=(ctx, head),
        device_id_type=MESH,
    )


def backward_kernel(
    n_ctx,
    n_head,
    seq_ref,
    lower_ref,
    q_hbm,
    k_hbm,
    v_hbm,
    do_hbm,
    dq_hbm,
    dk_ref,
    dv_ref,
    qs,
    dos,
    kv,
    role_k,
    role_v,
    acc,
    p_scr,
    dp_scr,
    m_scr,
    l_scr,
    d_scr,
    dq_acc,
    dq_out,
    g1_out,
    g1_in,
    prev_out,
    own_out,
    got_z,
    got_x,
    swap_out,
    swap_in,
    load_sem,
    own_sem,
    store_sem,
    send_k,
    recv_k,
    send_p,
    recv_p,
    send_f,
    recv_f,
    send_g,
    recv_g,
    send_z,
    recv_z,
    send_x,
    recv_x,
    send_s,
    recv_s,
):
    me = lax.axis_index("ctx")
    head = lax.axis_index("head")
    core = lax.rem(me, 2)
    partner = me + 1 - 2 * core
    after = lax.rem(me + 2, n_ctx)
    before = lax.rem(me + n_ctx - 2, n_ctx)
    others = [lax.rem(head + s, n_head) for s in range(1, n_head)]
    part = ROWS // n_head

    loads = []
    for which, src in ((0, k_hbm), (1, v_hbm)):
        cp = pltpu.make_async_copy(src, kv.at[0, which], own_sem.at[which])
        cp.start()
        loads.append(cp)
    for t in range(TILES):
        for h in range(HEADS):
            for i, (src, dst) in enumerate(((q_hbm, qs), (do_hbm, dos))):
                cp = pltpu.make_async_copy(
                    src.at[pl.ds(t * QT, QT), pl.ds(h * WIDTH, WIDTH)], dst.at[t, pl.ds(h * QT, QT)], load_sem.at[i, t, h]
                )
                cp.start()
                loads.append(cp)

    barrier = pltpu.get_barrier_semaphore()
    senders = [(partner, head), (before, head), (after, head)] + [(after, x) for x in others] + [(me, x) for x in others]
    for ctx, x in senders:
        pl.semaphore_signal(barrier, inc=1, device_id=(ctx, x), device_id_type=MESH)
    pl.semaphore_wait(barrier, len(senders))

    far = []
    for r in range(HALVES):
        for which, src in ((0, k_hbm), (1, v_hbm)):
            rows = pl.ds(r * HALF, HALF)
            i = 2 * r + which
            cp = copy_to(src.at[rows], kv.at[2 + core, which, rows], send_k.at[i], recv_k.at[i], after, head)
            cp.start()
            far.append(cp)
    near = []
    for which, src in ((0, k_hbm), (1, v_hbm)):
        cp = copy_to(src, kv.at[1, which], send_p.at[which], recv_p.at[which], partner, head)
        cp.start()
        near.append(cp)

    own = seq_ref[me]
    odd = lax.rem(own, 2) == 1
    core_is_first = seq_ref[before - core] == own - lax.rem(own, 2) - 2
    base = (own - 2) * ROWS
    stats = (p_scr, dp_scr, m_scr, l_scr, d_scr)
    for cp in loads:
        cp.wait()
    for t in range(TILES):
        n = (t + 1) * QT
        pass_one(0, t, 0, n, kv[0, 0, :n], kv[0, 1, :n], qs[t], dos[t], lower_ref, base, *stats)

    forwards = []
    for r in range(HALVES):
        for which in range(2):
            i = 2 * r + which
            rows = pl.ds(r * HALF, HALF)
            far[i].wait_recv()
            cp = copy_to(
                kv.at[2 + core, which, rows], kv.at[2 + core, which, rows], send_f.at[i], recv_f.at[i], partner, head
            )
            cp.start()
            forwards.append(cp)
    for cp in near + forwards:
        cp.wait_recv()
    for which, dst in ((0, role_k), (1, role_v)):
        even_rows = jnp.where(core_is_first, kv[2, which], kv[3, which])
        odd_rows = jnp.where(core_is_first, kv[3, which], kv[2, which])
        dst[0] = jnp.where(odd, kv[1, which], odd_rows)
        dst[1] = jnp.where(odd, odd_rows, even_rows)

    def one(t, _):
        pass_one(1, t, 0, ROWS, role_k[0], role_v[0], qs[t], dos[t], lower_ref, base, *stats)
        return 0

    lax.fori_loop(0, TILES, one, 0)
    for t in range(TILES):
        f = t * QT
        n = ROWS - f
        pass_one(2, t, f, n, role_k[1, f:], role_v[1, f:], qs[t], dos[t], lower_ref, base, *stats)
    acc[...] = jnp.zeros_like(acc)

    def grads(role):
        return jnp.concatenate([acc[role, :, :WIDTH] * SCALE, acc[role, :, WIDTH:]], axis=1)

    def two(t, _):
        dk, dv = pass_two(1, t, 0, ROWS, role_k[0], qs[t], dos[t], *stats, dq_acc)
        acc[1, :, :WIDTH] += dk
        acc[1, :, WIDTH:] += dv
        return 0

    lax.fori_loop(0, TILES, two, 0)
    g1_out[...] = grads(1).astype(jnp.bfloat16)
    trade = copy_to(g1_out, g1_in, send_g, recv_g, partner, head)
    trade.start()
    for t in range(TILES):
        f = t * QT
        n = ROWS - f
        dk, dv = pass_two(2, t, f, n, role_k[1, f:], qs[t], dos[t], *stats, dq_acc)
        acc[2, f:, :WIDTH] += dk
        acc[2, f:, WIDTH:] += dv
    trade.wait_recv()
    none = jnp.zeros((ROWS, 2 * WIDTH), jnp.float32)
    traded = g1_in[...].astype(jnp.float32)
    prev_out[...] = (grads(2) + jnp.where(odd, traded, none)).astype(jnp.bfloat16)
    back = []
    for s in range(n_head):
        x = lax.rem(head + s, n_head)
        cp = copy_to(prev_out.at[pl.ds(x * part, part)], got_z.at[s], send_z.at[s], recv_z.at[s], before, x)
        cp.start()
        back.append(cp)
    stores = []
    for t in range(TILES):
        n = (t + 1) * QT
        dk, dv = pass_two(0, t, 0, n, kv[0, 0, :n], qs[t], dos[t], *stats, dq_acc)
        acc[0, :n, :WIDTH] += dk
        acc[0, :n, WIDTH:] += dv
        rows = pl.ds(t * QT, QT)
        for h in range(HEADS):
            piece = dq_acc[t, :, h * QT : (h + 1) * QT] * SCALE
            dq_out[rows, h * WIDTH : (h + 1) * WIDTH] = piece.T.astype(dq_out.dtype)
        cp = pltpu.make_async_copy(dq_out.at[rows], dq_hbm.at[rows], store_sem.at[t])
        cp.start()
        stores.append(cp)
    acc[0] = grads(0) + jnp.where(odd, none, g1_in[...].astype(jnp.float32))
    own_out[...] = acc[0].astype(jnp.bfloat16)
    across = []
    for s in range(1, n_head):
        x = lax.rem(head + s, n_head)
        cp = copy_to(own_out.at[pl.ds(x * part, part)], got_x.at[s - 1], send_x.at[s - 1], recv_x.at[s - 1], me, x)
        cp.start()
        across.append(cp)
    for cp in back:
        cp.wait_recv()
    came = got_z[0].astype(jnp.float32)
    for s in range(1, n_head):
        came = came + got_z[s].astype(jnp.float32)
    swap_out[...] = came.astype(jnp.bfloat16)
    swap = copy_to(swap_out, swap_in, send_s, recv_s, partner, head)
    swap.start()
    total = acc[0, pl.ds(head * part, part), :]
    for cp in across:
        cp.wait_recv()
    for s in range(n_head - 1):
        total = total + got_x[s].astype(jnp.float32)
    swap.wait_recv()
    straight = lax.rem(seq_ref[after], 2) == lax.rem(own, 2)
    total = total + jnp.where(straight, came, swap_in[...].astype(jnp.float32))
    dk_ref[...] = total[:, :WIDTH].astype(jnp.bfloat16)
    dv_ref[...] = total[:, WIDTH:].astype(jnp.bfloat16)
    for cp in stores:
        cp.wait()
    for cp in far + near + forwards + [trade] + back + across + [swap]:
        cp.wait_send()


def shards(queries, keys, values, out_grad, doc_start, block_seq):
    n_ctx = lax.axis_size("ctx")
    n_head = lax.axis_size("head")
    part = ROWS // n_head
    smem = pl.BlockSpec(memory_space=pltpu.SMEM)
    vmem = pl.BlockSpec(memory_space=pltpu.VMEM)
    hbm = pl.BlockSpec(memory_space=pl.ANY)
    f32 = jnp.float32
    bf16 = jnp.bfloat16
    dma = pltpu.SemaphoreType.DMA
    return pl.pallas_call(
        functools.partial(backward_kernel, n_ctx, n_head),
        out_shape=(
            jax.ShapeDtypeStruct(queries.shape, bf16),
            jax.ShapeDtypeStruct((part, WIDTH), bf16),
            jax.ShapeDtypeStruct((part, WIDTH), bf16),
        ),
        in_specs=[smem, vmem, hbm, hbm, hbm, hbm],
        out_specs=(hbm, vmem, vmem),
        scratch_shapes=[
            pltpu.VMEM((TILES, COLS, WIDTH), bf16),
            pltpu.VMEM((TILES, COLS, WIDTH), bf16),
            pltpu.VMEM((4, 2, ROWS, WIDTH), bf16),
            pltpu.VMEM((2, ROWS, WIDTH), bf16),
            pltpu.VMEM((2, ROWS, WIDTH), bf16),
            pltpu.VMEM((3, ROWS, 2 * WIDTH), f32),
            pltpu.VMEM((3, TILES, ROWS, COLS), f32),
            pltpu.VMEM((3, TILES, ROWS, COLS), f32),
            pltpu.VMEM((3, TILES, 1, COLS), f32),
            pltpu.VMEM((TILES, 1, COLS), f32),
            pltpu.VMEM((TILES, 1, COLS), f32),
            pltpu.VMEM((TILES, WIDTH, COLS), f32),
            pltpu.VMEM((ROWS, HEADS * WIDTH), bf16),
            pltpu.VMEM((ROWS, 2 * WIDTH), bf16),
            pltpu.VMEM((ROWS, 2 * WIDTH), bf16),
            pltpu.VMEM((ROWS, 2 * WIDTH), bf16),
            pltpu.VMEM((ROWS, 2 * WIDTH), bf16),
            pltpu.VMEM((n_head, part, 2 * WIDTH), bf16),
            pltpu.VMEM((n_head - 1, part, 2 * WIDTH), bf16),
            pltpu.VMEM((part, 2 * WIDTH), bf16),
            pltpu.VMEM((part, 2 * WIDTH), bf16),
            dma((2, TILES, HEADS)),
            dma((2,)),
            dma((TILES,)),
            dma((4,)),
            dma((4,)),
            dma((2,)),
            dma((2,)),
            dma((4,)),
            dma((4,)),
            dma,
            dma,
            dma((n_head,)),
            dma((n_head,)),
            dma((n_head - 1,)),
            dma((n_head - 1,)),
            dma,
            dma,
        ],
        compiler_params=pltpu.CompilerParams(
            collective_id=0, has_side_effects=True, vmem_limit_bytes=VMEM_LIMIT
        ),
        name="backward",
    )(block_seq, doc_start.reshape(TILES, QT), queries, keys, values, out_grad)


def solution(mesh):
    return jax.shard_map(
        shards,
        mesh=mesh,
        in_specs=(
            P("ctx", "head"),
            P("ctx", None),
            P("ctx", None),
            P("ctx", "head"),
            P("ctx"),
            P(),
        ),
        out_specs=(P("ctx", "head"), P(("ctx", "head"), None), P(("ctx", "head"), None)),
        check_vma=False,
    )
```

time: 128 us -> 42.8 us (0.33); the launches traced: 126 us -> 42.5 us
  waiting for transfers between devices: 40.5 us -> 0 us
  Pallas kernels: 0 us -> 38.6 us
  starting transfers between devices: 24.7 us -> 0 us
  matrix products: 21.7 us -> 0 us
  between operations: 18.4 us -> 0.65 us
  other arithmetic: 13 us -> 0 us
  local copies, waits for them, and re-layouts: 8.04 us -> 3.26 us
    pallas_call x0 -> x1, Pallas kernels: none -> 38.6 us  [shards(): pl.pallas_call(functools.partial(backward_kernel, n_ctx, n_head), out_sha...]
    ppermute x8 -> x0, starting transfers between devices: 24.6 us -> none  [passed_along(): return lax.ppermute(block, axis, route)]
    reduce_scatter x1 -> x0, waiting for transfers between devices: 24.6 us -> none  [shards(): lax.psum_scatter(total.astype(jnp.bfloat16), 'head', scatter_dimension=0,...]
    dot_general x20 -> x0, matrix products: 21.7 us -> none  [the longest x16 18.6 us: contract_rows(): lax.dot_general(left_side, right_side, (((left_axis,), (right_axis,)), ((...]
    ppermute x8 -> x0, waiting for transfers between devices: 15.9 us -> none  [passed_along(): return lax.ppermute(block, axis, route)]
    reduce_sum x4 -> x0, other arithmetic: 6.08 us -> none  [the longest x2 2.73 us: shards(): probability = weight / jnp.sum(weight, axis=1, keepdims=True)]
    slice x4 -> x0, local copies, waits for them, and re-layouts: 4.87 us -> none  [the longest x3 3.47 us: shards(): grads[back_step * row_count:(back_step + 1) * row_count][None]]
    convert_element_type x4 -> x0, other arithmetic: 3.34 us -> none  [the longest x1 2.45 us: shards(): score_grad = (probability * (prob_grad - row_delta)).astype(jnp.bfloat16)]
  transfers between devices with their start and end apart: 9 -> 0, of which waited for: 4 -> 0; matrix products, arithmetic and copies ran while one was open for 6% -> 0% of each run, Pallas kernels for 0% -> 0%
where the time goes in v2:
time: 42.8 us; the launch traced here: 42.5 us
  Pallas kernels  38.6 us (90%)
  local copies, waits for them, and re-layouts  3.26 us (8%)
  between operations  0.65 us (2%)
    pallas_call x1, Pallas kernels, shards(): pl.pallas_call(functools.partial(backward_kernel, n_ctx, n_head), out_sha...  38.6 us
    unnamed x7, local copies, waits for them, and re-layouts  3.26 us

profile of v2, /device:TPU:1, one launch (start us, length us, event | category | flops | bytes accessed | tf_op | source)
XLA Modules:
  0.0 42.5 jit_solution(12628919741342231762)
XLA Ops:
  0.6 38.6 %backward.1 = (bf16[512,512]{1,0:T(8,128)(2,1)}, bf16[128,128]{1,0:T(8,128)(2,1)}, bf16[128,128]{1,0:T(8,128)(2,1)}) custom-call(s32[64]{0:T(128)} %seq_ref.1, s32[4,128]{1,0:T(4,128)} %bitcast.1, bf16[512,512]{1,0:T(8,128)(2,1)} %q_hbm.1, bf16[512,128]{1,0:T(8,128)(2,1)} %k_hbm.1, bf16[512,128]{1,0:T(8,128)(2,1)} %v_hbm.1, bf16[512,512]{1,0:T(8,128)(2,1)} %do_hbm.1), custom_call_target="tpu_custom_call" | custom-call | tf_op jit(solution)/shard_map/backward/pallas_call | solution.py:312
  39.3 0.0 copy-start.1
  39.3 1.9 %copy.12 = bf16[512,512]{1,0:T(8,128)(2,1)} copy(bf16[512,512]{1,0:T(8,128)(2,1)} %get-tuple-element.6) | data formatting | bytes 1048576
  41.2 0.0 copy-done.1
  41.2 0.0 copy-start
  41.2 0.6 %copy.13 = bf16[128,128]{1,0:T(8,128)(2,1)} copy(bf16[128,128]{1,0:T(8,128)(2,1)S(1)} %copy-done.1) | data formatting | bytes 65536
  41.8 0.2 copy-done
  41.9 0.6 %copy.14 = bf16[128,128]{1,0:T(8,128)(2,1)} copy(bf16[128,128]{1,0:T(8,128)(2,1)S(1)} %copy-done) | data formatting | bytes 65536
Async XLA Ops:
  39.3 1.9 %copy-start.1 = (bf16[128,128]{1,0:T(8,128)(2,1)S(1)}, bf16[128,128]{1,0:T(8,128)(2,1)}, u32[]{:S(2)}) copy-start(bf16[128,128]{1,0:T(8,128)(2,1)} %get-tuple-element.7) | copy-start | bytes 98308
  41.2 0.8 %copy-start = (bf16[128,128]{1,0:T(8,128)(2,1)S(1)}, bf16[128,128]{1,0:T(8,128)(2,1)}, u32[]{:S(2)}) copy-start(bf16[128,128]{1,0:T(8,128)(2,1)} %get-tuple-element.8) | copy-start | bytes 98308

commit v3 on v2

v3 whole, which is shorter than its diff:
```python
import functools
import math

import jax
import jax.numpy as jnp
from jax import lax
from jax.experimental import pallas as pl
from jax.experimental.pallas import tpu as pltpu
from jax.sharding import PartitionSpec as P

MESH = pl.DeviceIdType.MESH

ROWS = 512
WIDTH = 128
HEADS = 4
QT = 128
TILES = ROWS // QT
COLS = HEADS * QT
MASKED = -1e30
CHUNKS = TILES
VMEM_LIMIT = 59 * 1024 * 1024 + 512 * 1024
SCALE = WIDTH ** (-0.5)
SCALE2 = SCALE * math.log2(math.e)


def dot(a, b, ca, cb):
    return lax.dot_general(a, b, (((ca,), (cb,)), ((), ())), preferred_element_type=jnp.float32)


def update(step, t, k, v, q, do, key_pos, causal, lower_ref, base, p_dst, dp_dst, m_scr, l_scr, d_scr):
    row_pos = 2 * ROWS + t * QT + lax.broadcasted_iota(jnp.int32, (1, QT), 1)
    lower = jnp.clip(lower_ref[pl.ds(t, 1), :] - base, jnp.maximum(row_pos - 2 * ROWS + 1, -base), row_pos)
    seen = key_pos >= lower
    if causal:
        seen = seen & (key_pos <= row_pos)
    bias = jnp.where(seen, 0.0, MASKED)
    s = dot(k, q, 1, 1) * SCALE2 + jnp.concatenate([bias] * HEADS, axis=1)
    dp = dot(v, do, 1, 1)
    m = jnp.max(s, axis=0, keepdims=True)
    if step > 0:
        m_old = m_scr[step - 1, t]
        m = jnp.maximum(m_old, m)
        shrink = jnp.exp2(m_old - m)
    p = jnp.exp2(s - m)
    l = jnp.sum(p, axis=0, keepdims=True)
    d = jnp.sum(p * dp, axis=0, keepdims=True)
    if step > 0:
        l = l + l_scr[t] * shrink
        d = d + d_scr[t] * shrink
    m_scr[step, t] = m
    l_scr[t] = l
    d_scr[t] = d
    p_dst[...] = p
    dp_dst[...] = dp


def key_grads(p, dp, factor, delta, q, do, ds_dst):
    n = ds_dst.shape[0]
    p = (p * factor).reshape(n, COLS)
    ds = (p * (dp.reshape(n, COLS) - delta)).astype(jnp.bfloat16)
    ds_dst[...] = ds
    return dot(ds, q, 1, 0), dot(p.astype(jnp.bfloat16), do, 1, 0)


def copy_to(src, dst, send, recv, ctx, head):
    return pltpu.make_async_remote_copy(
        src_ref=src,
        dst_ref=dst,
        send_sem=send,
        recv_sem=recv,
        device_id=(ctx, head),
        device_id_type=MESH,
    )


def backward_kernel(
    n_ctx,
    n_head,
    seq_ref,
    lower_ref,
    q_hbm,
    k_hbm,
    v_hbm,
    do_hbm,
    dq_out,
    dk_ref,
    dv_ref,
    qs,
    dos,
    kv,
    role_k,
    role_v,
    acc,
    p_own,
    dp_own,
    p_far,
    dp_far,
    ds_0,
    ds_1,
    ds_2,
    m_scr,
    l_scr,
    d_scr,
    g1_out,
    g1_in,
    prev_out,
    own_out,
    got_z,
    got_x,
    swap_out,
    swap_in,
    load_sem,
    own_sem,
    send_k,
    recv_k,
    send_p,
    recv_p,
    send_f,
    recv_f,
    send_g,
    recv_g,
    send_z,
    recv_z,
    send_x,
    recv_x,
    send_s,
    recv_s,
):
    me = lax.axis_index("ctx")
    head = lax.axis_index("head")
    core = lax.rem(me, 2)
    partner = me + 1 - 2 * core
    after = lax.rem(me + 2, n_ctx)
    before = lax.rem(me + n_ctx - 2, n_ctx)
    others = [lax.rem(head + s, n_head) for s in range(1, n_head)]
    part = ROWS // n_head

    loads = []
    for which, src in ((0, k_hbm), (1, v_hbm)):
        cp = pltpu.make_async_copy(src, kv.at[0, which], own_sem.at[which])
        cp.start()
        loads.append(cp)
    for t in range(TILES):
        for h in range(HEADS):
            for i, (src, dst) in enumerate(((q_hbm, qs), (do_hbm, dos))):
                cp = pltpu.make_async_copy(
                    src.at[pl.ds(t * QT, QT), pl.ds(h * WIDTH, WIDTH)], dst.at[t, pl.ds(h * QT, QT)], load_sem.at[i, t, h]
                )
                cp.start()
                loads.append(cp)

    barrier = pltpu.get_barrier_semaphore()
    senders = [(partner, head), (before, head), (after, head)] + [(after, x) for x in others] + [(me, x) for x in others]
    for ctx, x in senders:
        pl.semaphore_signal(barrier, inc=1, device_id=(ctx, x), device_id_type=MESH)
    pl.semaphore_wait(barrier, len(senders))

    far = []
    for r in range(CHUNKS):
        for which, src in ((0, k_hbm), (1, v_hbm)):
            rows = pl.ds(r * QT, QT)
            i = 2 * r + which
            cp = copy_to(src.at[rows], kv.at[2 + core, which, rows], send_k.at[i], recv_k.at[i], after, head)
            cp.start()
            far.append(cp)
    near = []
    for which, src in ((0, k_hbm), (1, v_hbm)):
        cp = copy_to(src, kv.at[1, which], send_p.at[which], recv_p.at[which], partner, head)
        cp.start()
        near.append(cp)

    own = seq_ref[me]
    odd = lax.rem(own, 2) == 1
    core_is_first = seq_ref[before - core] == own - lax.rem(own, 2) - 2
    base = (own - 2) * ROWS
    stats = (m_scr, l_scr, d_scr)
    for cp in loads:
        cp.wait()
    for t in range(TILES):
        n = (t + 1) * QT
        key_pos = 2 * ROWS + lax.broadcasted_iota(jnp.int32, (n, QT), 0)
        update(
            0, t, kv[0, 0, :n], kv[0, 1, :n], qs[t], dos[t], key_pos, True, lower_ref, base,
            p_own.at[t, pl.ds(0, n)], dp_own.at[t, pl.ds(0, n)], *stats,
        )

    forwards = []

    def pass_on(r):
        rows = pl.ds(r * QT, QT)
        for which in range(2):
            i = 2 * r + which
            far[i].wait_recv()
            place = kv.at[2 + core, which, rows]
            cp = copy_to(place, place, send_f.at[i], recv_f.at[i], partner, head)
            cp.start()
            forwards.append(cp)

    pass_on(0)
    for cp in near:
        cp.wait_recv()
    for r in range(CHUNKS):
        if r + 1 < CHUNKS:
            pass_on(r + 1)
        rows = slice(r * QT, (r + 1) * QT)
        for which, dst in ((0, role_k), (1, role_v)):
            forwards[2 * r + which].wait_recv()
            even_rows = jnp.where(core_is_first, kv[2, which, rows], kv[3, which, rows])
            odd_rows = jnp.where(core_is_first, kv[3, which, rows], kv[2, which, rows])
            dst[r, :QT] = jnp.where(odd, kv[1, which, rows], odd_rows)
            dst[r, QT:] = jnp.where(odd, odd_rows, even_rows)
        for t in range(TILES):
            n = 2 * QT if t <= r else QT
            row = lax.broadcasted_iota(jnp.int32, (n, QT), 0)
            key_pos = r * QT + row + jnp.where(row < QT, ROWS, -QT)
            update(
                r + 1, t, role_k[r, :n], role_v[r, :n], qs[t], dos[t], key_pos, False, lower_ref, base,
                p_far.at[r, t, pl.ds(0, n)], dp_far.at[r, t, pl.ds(0, n)], *stats,
            )

    for t in range(TILES):
        inv = 1.0 / l_scr[t]
        l_scr[t] = inv
        d_scr[t] = d_scr[t] * inv
    for t in range(TILES):
        factor = jnp.exp2(m_scr[1:, t] - m_scr[CHUNKS, t][None]) * l_scr[t][None]
        dk, dv = key_grads(p_far[:, t, :QT], dp_far[:, t, :QT], factor, d_scr[t], qs[t], dos[t], ds_1.at[t])
        if t == 0:
            acc[1, :, :WIDTH] = dk
            acc[1, :, WIDTH:] = dv
        else:
            acc[1, :, :WIDTH] += dk
            acc[1, :, WIDTH:] += dv

    def grads(role):
        return jnp.concatenate([acc[role, :, :WIDTH] * SCALE, acc[role, :, WIDTH:]], axis=1)

    g1_out[...] = grads(1).astype(jnp.bfloat16)
    trade = copy_to(g1_out, g1_in, send_g, recv_g, partner, head)
    trade.start()
    for t in range(TILES):
        f = t * QT
        factor = jnp.exp2(m_scr[1 + t :, t] - m_scr[CHUNKS, t][None]) * l_scr[t][None]
        dk, dv = key_grads(
            p_far[t:, t, QT:], dp_far[t:, t, QT:], factor, d_scr[t], qs[t], dos[t], ds_2.at[t, pl.ds(f, ROWS - f)]
        )
        if t == 0:
            acc[2, :, :WIDTH] = dk
            acc[2, :, WIDTH:] = dv
        else:
            acc[2, f:, :WIDTH] += dk
            acc[2, f:, WIDTH:] += dv
    trade.wait_recv()
    none = jnp.zeros((ROWS, 2 * WIDTH), jnp.float32)
    traded = g1_in[...].astype(jnp.float32)
    prev_out[...] = (grads(2) + jnp.where(odd, traded, none)).astype(jnp.bfloat16)
    back = []
    for s in range(n_head):
        x = lax.rem(head + s, n_head)
        cp = copy_to(prev_out.at[pl.ds(x * part, part)], got_z.at[s], send_z.at[s], recv_z.at[s], before, x)
        cp.start()
        back.append(cp)
    for t in reversed(range(TILES)):
        n = (t + 1) * QT
        factor = jnp.exp2(m_scr[0, t] - m_scr[CHUNKS, t]) * l_scr[t]
        dk, dv = key_grads(
            p_own[t, :n], dp_own[t, :n], factor, d_scr[t], qs[t], dos[t], ds_0.at[t, pl.ds(0, n)]
        )
        if t == TILES - 1:
            acc[0, :, :WIDTH] = dk
            acc[0, :, WIDTH:] = dv
        else:
            acc[0, :n, :WIDTH] += dk
            acc[0, :n, WIDTH:] += dv
    acc[0] = grads(0) + jnp.where(odd, none, g1_in[...].astype(jnp.float32))
    own_out[...] = acc[0].astype(jnp.bfloat16)
    across = []
    for s in range(1, n_head):
        x = lax.rem(head + s, n_head)
        cp = copy_to(own_out.at[pl.ds(x * part, part)], got_x.at[s - 1], send_x.at[s - 1], recv_x.at[s - 1], me, x)
        cp.start()
        across.append(cp)
    for t in range(TILES):
        n = (t + 1) * QT
        f = t * QT
        k1 = role_k[:, :QT].reshape(ROWS, WIDTH)
        k2 = role_k[t:, QT:].reshape(ROWS - f, WIDTH)
        dq = dot(kv[0, 0, :n], ds_0[t, :n], 0, 0) + dot(k1, ds_1[t], 0, 0) + dot(k2, ds_2[t, f:], 0, 0)
        dq = dq * SCALE
        rows = pl.ds(t * QT, QT)
        for h in range(HEADS):
            dq_out[rows, h * WIDTH : (h + 1) * WIDTH] = dq[:, h * QT : (h + 1) * QT].T.astype(dq_out.dtype)
    for cp in back:
        cp.wait_recv()
    came = got_z[0].astype(jnp.float32)
    for s in range(1, n_head):
        came = came + got_z[s].astype(jnp.float32)
    swap_out[...] = came.astype(jnp.bfloat16)
    swap = copy_to(swap_out, swap_in, send_s, recv_s, partner, head)
    swap.start()
    total = acc[0, pl.ds(head * part, part), :]
    for cp in across:
        cp.wait_recv()
    for s in range(n_head - 1):
        total = total + got_x[s].astype(jnp.float32)
    swap.wait_recv()
    straight = lax.rem(seq_ref[after], 2) == lax.rem(own, 2)
    total = total + jnp.where(straight, came, swap_in[...].astype(jnp.float32))
    dk_ref[...] = total[:, :WIDTH].astype(jnp.bfloat16)
    dv_ref[...] = total[:, WIDTH:].astype(jnp.bfloat16)
    for cp in far + near + forwards + [trade] + back + across + [swap]:
        cp.wait_send()


def hand_on_kernel(dq_ref, dk_ref, dv_ref, dq_out, dk_out, dv_out, sem):
    copies = []
    for i, (src, dst) in enumerate(((dq_ref, dq_out), (dk_ref, dk_out), (dv_ref, dv_out))):
        cp = pltpu.make_async_copy(src, dst, sem.at[i])
        cp.start()
        copies.append(cp)
    for cp in copies:
        cp.wait()


def shards(queries, keys, values, out_grad, doc_start, block_seq):
    n_ctx = lax.axis_size("ctx")
    n_head = lax.axis_size("head")
    part = ROWS // n_head
    smem = pl.BlockSpec(memory_space=pltpu.SMEM)
    vmem = pl.BlockSpec(memory_space=pltpu.VMEM)
    hbm = pl.BlockSpec(memory_space=pltpu.HBM)
    f32 = jnp.float32
    bf16 = jnp.bfloat16
    dma = pltpu.SemaphoreType.DMA
    grads = pl.pallas_call(
        functools.partial(backward_kernel, n_ctx, n_head),
        out_shape=(
            pltpu.VMEM(queries.shape, bf16),
            pltpu.VMEM((part, WIDTH), bf16),
            pltpu.VMEM((part, WIDTH), bf16),
        ),
        in_specs=[smem, vmem, hbm, hbm, hbm, hbm],
        out_specs=(vmem, vmem, vmem),
        scratch_shapes=[
            pltpu.VMEM((TILES, COLS, WIDTH), bf16),
            pltpu.VMEM((TILES, COLS, WIDTH), bf16),
            pltpu.VMEM((4, 2, ROWS, WIDTH), bf16),
            pltpu.VMEM((CHUNKS, 2 * QT, WIDTH), bf16),
            pltpu.VMEM((CHUNKS, 2 * QT, WIDTH), bf16),
            pltpu.VMEM((3, ROWS, 2 * WIDTH), f32),
            pltpu.VMEM((TILES, ROWS, COLS), f32),
            pltpu.VMEM((TILES, ROWS, COLS), f32),
            pltpu.VMEM((CHUNKS, TILES, 2 * QT, COLS), f32),
            pltpu.VMEM((CHUNKS, TILES, 2 * QT, COLS), f32),
            pltpu.VMEM((TILES, ROWS, COLS), bf16),
            pltpu.VMEM((TILES, ROWS, COLS), bf16),
            pltpu.VMEM((TILES, ROWS, COLS), bf16),
            pltpu.VMEM((CHUNKS + 1, TILES, 1, COLS), f32),
            pltpu.VMEM((TILES, 1, COLS), f32),
            pltpu.VMEM((TILES, 1, COLS), f32),
            pltpu.VMEM((ROWS, 2 * WIDTH), bf16),
            pltpu.VMEM((ROWS, 2 * WIDTH), bf16),
            pltpu.VMEM((ROWS, 2 * WIDTH), bf16),
            pltpu.VMEM((ROWS, 2 * WIDTH), bf16),
            pltpu.VMEM((n_head, part, 2 * WIDTH), bf16),
            pltpu.VMEM((n_head - 1, part, 2 * WIDTH), bf16),
            pltpu.VMEM((part, 2 * WIDTH), bf16),
            pltpu.VMEM((part, 2 * WIDTH), bf16),
            dma((2, TILES, HEADS)),
            dma((2,)),
            dma((2 * CHUNKS,)),
            dma((2 * CHUNKS,)),
            dma((2,)),
            dma((2,)),
            dma((2 * CHUNKS,)),
            dma((2 * CHUNKS,)),
            dma,
            dma,
            dma((n_head,)),
            dma((n_head,)),
            dma((n_head - 1,)),
            dma((n_head - 1,)),
            dma,
            dma,
        ],
        compiler_params=pltpu.CompilerParams(
            collective_id=0, has_side_effects=True, vmem_limit_bytes=VMEM_LIMIT
        ),
        name="backward",
    )(block_seq, doc_start.reshape(TILES, QT), queries, keys, values, out_grad)
    return pl.pallas_call(
        hand_on_kernel,
        out_shape=tuple(jax.ShapeDtypeStruct(g.shape, g.dtype) for g in grads),
        in_specs=[vmem] * 3,
        out_specs=(hbm,) * 3,
        scratch_shapes=[dma((3,))],
        compiler_params=pltpu.CompilerParams(vmem_limit_bytes=1024 * 1024),
        name="hand_on",
    )(*grads)


def solution(mesh):
    return jax.shard_map(
        shards,
        mesh=mesh,
        in_specs=(
            P("ctx", "head"),
            P("ctx", None),
            P("ctx", None),
            P("ctx", "head"),
            P("ctx"),
            P(),
        ),
        out_specs=(P("ctx", "head"), P(("ctx", "head"), None), P(("ctx", "head"), None)),
        check_vma=False,
    )
```

time: 42.8 us -> 36.3 us (0.85)
  local copies, waits for them, and re-layouts: 3.26 us -> 0 us
  Pallas kernels: 38.6 us -> 35.5 us
    pallas_call x1, Pallas kernels: 38.6 us -> 34.7 us  [shards(): pl.pallas_call(functools.partial(backward_kernel, n_ctx, n_head), out_sha...]
    unnamed x7 -> x0, local copies, waits for them, and re-layouts: 3.26 us -> none
    pallas_call x0 -> x1, Pallas kernels: none -> 0.83 us  [shards(): pl.pallas_call(hand_on_kernel, out_shape=tuple((jax.ShapeDtypeStruct(g.sh...]
where the time goes in v3:
time: 36.3 us; the launch traced here: 36.1 us
  Pallas kernels  35.5 us (98%)
  between operations  0.64 us (2%)
    pallas_call x1, Pallas kernels, shards(): pl.pallas_call(functools.partial(backward_kernel, n_ctx, n_head), out_sha...  34.7 us
    pallas_call x1, Pallas kernels, shards(): pl.pallas_call(hand_on_kernel, out_shape=tuple((jax.ShapeDtypeStruct(g.sh...  0.83 us

profile of v3, /device:TPU:1, one launch (start us, length us, event | category | flops | bytes accessed | tf_op | source)
XLA Modules:
  0.0 36.1 jit_solution(2637445105248865973)
XLA Ops:
  0.6 34.7 %backward.1 = (bf16[512,512]{1,0:T(8,128)(2,1)S(1)}, bf16[128,128]{1,0:T(8,128)(2,1)S(1)}, bf16[128,128]{1,0:T(8,128)(2,1)S(1)}) custom-call(s32[64]{0:T(128)} %seq_ref.1, s32[4,128]{1,0:T(4,128)} %bitcast.1, bf16[512,512]{1,0:T(8,128)(2,1)} %q_hbm.1, bf16[512,128]{1,0:T(8,128)(2,1)} %k_hbm.1, bf16[512,128]{1,0:T(8,128)(2,1)} %v_hbm.1, bf16[512,512]{1,0:T(8,128)(2,1)} %do_hbm.1), custom_call_target="tpu_custom_call" | custom-call | tf_op jit(solution)/shard_map/backward/pallas_call | solution.py:335
  35.3 0.8 %hand_on.1 = (bf16[512,512]{1,0:T(8,128)(2,1)}, bf16[128,128]{1,0:T(8,128)(2,1)}, bf16[128,128]{1,0:T(8,128)(2,1)}) custom-call(bf16[512,512]{1,0:T(8,128)(2,1)S(1)} %get-tuple-element.6.dq_ref, bf16[128,128]{1,0:T(8,128)(2,1)S(1)} %get-tuple-element.7.dk_ref, bf16[128,128]{1,0:T(8,128)(2,1)S(1)} %get-tuple-element.8.dv_ref), custom_call_target="tpu_custom_call" | custom-call | tf_op jit(solution)/shard_map/hand_on/pallas_call | solution.py:391

commit v4 on v3

--- a/solution.py
+++ b/solution.py
@@ -18,6 +18,7 @@
 COLS = HEADS * QT
 MASKED = -1e30
 CHUNKS = TILES
+STRAIGHT = 80
 VMEM_LIMIT = 59 * 1024 * 1024 + 512 * 1024
 SCALE = WIDTH ** (-0.5)
 SCALE2 = SCALE * math.log2(math.e)
@@ -106,6 +107,9 @@
     prev_out,
     own_out,
     got_z,
+    got_part,
+    rest_out,
+    got_rest,
     got_x,
     swap_out,
     swap_in,
@@ -125,6 +129,10 @@
     recv_x,
     send_s,
     recv_s,
+    send_part,
+    recv_part,
+    send_rest,
+    recv_rest,
 ):
     me = lax.axis_index("ctx")
     head = lax.axis_index("head")
@@ -135,24 +143,22 @@
     others = [lax.rem(head + s, n_head) for s in range(1, n_head)]
     part = ROWS // n_head
 
-    loads = []
-    for which, src in ((0, k_hbm), (1, v_hbm)):
-        cp = pltpu.make_async_copy(src, kv.at[0, which], own_sem.at[which])
-        cp.start()
-        loads.append(cp)
-    for t in range(TILES):
-        for h in range(HEADS):
-            for i, (src, dst) in enumerate(((q_hbm, qs), (do_hbm, dos))):
-                cp = pltpu.make_async_copy(
-                    src.at[pl.ds(t * QT, QT), pl.ds(h * WIDTH, WIDTH)], dst.at[t, pl.ds(h * QT, QT)], load_sem.at[i, t, h]
-                )
-                cp.start()
-                loads.append(cp)
-
     barrier = pltpu.get_barrier_semaphore()
     senders = [(partner, head), (before, head), (after, head)] + [(after, x) for x in others] + [(me, x) for x in others]
     for ctx, x in senders:
         pl.semaphore_signal(barrier, inc=1, device_id=(ctx, x), device_id_type=MESH)
+    loads = []
+    for src, dst, i in ((k_hbm, kv.at[0, 0], 0), (v_hbm, kv.at[0, 1], 1)):
+        cp = pltpu.make_async_copy(src, dst, own_sem.at[i])
+        cp.start()
+        loads.append(cp)
+    for h in range(HEADS):
+        for i, (src, dst) in enumerate(((q_hbm, qs), (do_hbm, dos))):
+            cp = pltpu.make_async_copy(
+                src.at[:, :, pl.ds(h * WIDTH, WIDTH)], dst.at[:, pl.ds(h * QT, QT), :], load_sem.at[i, h]
+            )
+            cp.start()
+            loads.append(cp)
     pl.semaphore_wait(barrier, len(senders))
 
     far = []
@@ -254,10 +260,18 @@
     none = jnp.zeros((ROWS, 2 * WIDTH), jnp.float32)
     traded = g1_in[...].astype(jnp.float32)
     prev_out[...] = (grads(2) + jnp.where(odd, traded, none)).astype(jnp.bfloat16)
+    summed = []
+    for s in range(1, n_head):
+        x = lax.rem(head + s, n_head)
+        some = pl.ds(pl.multiple_of(x * part + STRAIGHT, 16), part - STRAIGHT)
+        cp = copy_to(prev_out.at[some], got_part.at[s - 1], send_part.at[s - 1], recv_part.at[s - 1], me, x)
+        cp.start()
+        summed.append(cp)
     back = []
     for s in range(n_head):
         x = lax.rem(head + s, n_head)
-        cp = copy_to(prev_out.at[pl.ds(x * part, part)], got_z.at[s], send_z.at[s], recv_z.at[s], before, x)
+        some = pl.ds(pl.multiple_of(x * part, part), STRAIGHT)
+        cp = copy_to(prev_out.at[some], got_z.at[s], send_z.at[s], recv_z.at[s], before, x)
         cp.start()
         back.append(cp)
     for t in reversed(range(TILES)):
@@ -290,11 +304,22 @@
         rows = pl.ds(t * QT, QT)
         for h in range(HEADS):
             dq_out[rows, h * WIDTH : (h + 1) * WIDTH] = dq[:, h * QT : (h + 1) * QT].T.astype(dq_out.dtype)
+    for cp in summed:
+        cp.wait_recv()
+    some = pl.ds(pl.multiple_of(head * part + STRAIGHT, 16), part - STRAIGHT)
+    rest = prev_out[some, :].astype(jnp.float32)
+    for s in range(n_head - 1):
+        rest = rest + got_part[s].astype(jnp.float32)
+    rest_out[...] = rest.astype(jnp.bfloat16)
+    cp = copy_to(rest_out, got_rest, send_rest, recv_rest, before, head)
+    cp.start()
+    back.append(cp)
     for cp in back:
         cp.wait_recv()
     came = got_z[0].astype(jnp.float32)
     for s in range(1, n_head):
         came = came + got_z[s].astype(jnp.float32)
+    came = jnp.concatenate([came, got_rest[...].astype(jnp.float32)], axis=0)
     swap_out[...] = came.astype(jnp.bfloat16)
     swap = copy_to(swap_out, swap_in, send_s, recv_s, partner, head)
     swap.start()
@@ -308,7 +333,7 @@
     total = total + jnp.where(straight, came, swap_in[...].astype(jnp.float32))
     dk_ref[...] = total[:, :WIDTH].astype(jnp.bfloat16)
     dv_ref[...] = total[:, WIDTH:].astype(jnp.bfloat16)
-    for cp in far + near + forwards + [trade] + back + across + [swap]:
+    for cp in far + near + forwards + [trade] + summed + back + across + [swap]:
         cp.wait_send()
 
 
@@ -362,11 +387,14 @@
             pltpu.VMEM((ROWS, 2 * WIDTH), bf16),
             pltpu.VMEM((ROWS, 2 * WIDTH), bf16),
             pltpu.VMEM((ROWS, 2 * WIDTH), bf16),
-            pltpu.VMEM((n_head, part, 2 * WIDTH), bf16),
+            pltpu.VMEM((n_head, STRAIGHT, 2 * WIDTH), bf16),
+            pltpu.VMEM((n_head - 1, part - STRAIGHT, 2 * WIDTH), bf16),
+            pltpu.VMEM((part - STRAIGHT, 2 * WIDTH), bf16),
+            pltpu.VMEM((part - STRAIGHT, 2 * WIDTH), bf16),
             pltpu.VMEM((n_head - 1, part, 2 * WIDTH), bf16),
             pltpu.VMEM((part, 2 * WIDTH), bf16),
             pltpu.VMEM((part, 2 * WIDTH), bf16),
-            dma((2, TILES, HEADS)),
+            dma((2, HEADS)),
             dma((2,)),
             dma((2 * CHUNKS,)),
             dma((2 * CHUNKS,)),
@@ -382,12 +410,23 @@
             dma((n_head - 1,)),
             dma,
             dma,
+            dma((n_head - 1,)),
+            dma((n_head - 1,)),
+            dma,
+            dma,
         ],
         compiler_params=pltpu.CompilerParams(
             collective_id=0, has_side_effects=True, vmem_limit_bytes=VMEM_LIMIT
         ),
         name="backward",
-    )(block_seq, doc_start.reshape(TILES, QT), queries, keys, values, out_grad)
+    )(
+        block_seq,
+        doc_start.reshape(TILES, QT),
+        queries.reshape(TILES, QT, HEADS * WIDTH),
+        keys,
+        values,
+        out_grad.reshape(TILES, QT, HEADS * WIDTH),
+    )
     return pl.pallas_call(
         hand_on_kernel,
         out_shape=tuple(jax.ShapeDtypeStruct(g.shape, g.dtype) for g in grads),

time: 36.3 us -> 34.8 us (0.959)
  Pallas kernels: 35.5 us -> 34 us
    pallas_call x1, Pallas kernels: 34.7 us -> 33.2 us  [shards(): pl.pallas_call(functools.partial(backward_kernel, n_ctx, n_head), out_sha...]
where the time goes in v4:
time: 34.8 us; the launch traced here: 34.6 us
  Pallas kernels  34 us (98%)
  between operations  0.64 us (2%)
    pallas_call x1, Pallas kernels, shards(): pl.pallas_call(functools.partial(backward_kernel, n_ctx, n_head), out_sha...  33.2 us
    pallas_call x1, Pallas kernels, shards(): pl.pallas_call(hand_on_kernel, out_shape=tuple((jax.ShapeDtypeStruct(g.sh...  0.83 us

profile of v4, /device:TPU:1, one launch (start us, length us, event | category | flops | bytes accessed | tf_op | source)
XLA Modules:
  0.0 34.6 jit_solution(15332406817005487818)
XLA Ops:
  0.6 33.2 %backward.1 = (bf16[512,512]{1,0:T(8,128)(2,1)S(1)}, bf16[128,128]{1,0:T(8,128)(2,1)S(1)}, bf16[128,128]{1,0:T(8,128)(2,1)S(1)}) custom-call(s32[64]{0:T(128)} %seq_ref.1, s32[4,128]{1,0:T(4,128)} %bitcast.5, bf16[4,128,512]{2,1,0:T(8,128)(2,1)} %bitcast.3, bf16[512,128]{1,0:T(8,128)(2,1)} %k_hbm.1, bf16[512,128]{1,0:T(8,128)(2,1)} %v_hbm.1, ...), custom_call_target="tpu_custom_call" | custom-call | tf_op jit(solution)/shard_map/backward/pallas_call | solution.py:360
  33.8 0.8 %hand_on.1 = (bf16[512,512]{1,0:T(8,128)(2,1)}, bf16[128,128]{1,0:T(8,128)(2,1)}, bf16[128,128]{1,0:T(8,128)(2,1)}) custom-call(bf16[512,512]{1,0:T(8,128)(2,1)S(1)} %get-tuple-element.6.dq_ref, bf16[128,128]{1,0:T(8,128)(2,1)S(1)} %get-tuple-element.7.dk_ref, bf16[128,128]{1,0:T(8,128)(2,1)S(1)} %get-tuple-element.8.dv_ref), custom_call_target="tpu_custom_call" | custom-call | tf_op jit(solution)/shard_map/hand_on/pallas_call | solution.py:430

commit v5 on v4

--- a/solution.py
+++ b/solution.py
@@ -294,6 +294,16 @@
         cp = copy_to(own_out.at[pl.ds(x * part, part)], got_x.at[s - 1], send_x.at[s - 1], recv_x.at[s - 1], me, x)
         cp.start()
         across.append(cp)
+    for cp in summed:
+        cp.wait_recv()
+    some = pl.ds(pl.multiple_of(head * part + STRAIGHT, 16), part - STRAIGHT)
+    rest = prev_out[some, :].astype(jnp.float32)
+    for s in range(n_head - 1):
+        rest = rest + got_part[s].astype(jnp.float32)
+    rest_out[...] = rest.astype(jnp.bfloat16)
+    cp = copy_to(rest_out, got_rest, send_rest, recv_rest, before, head)
+    cp.start()
+    back.append(cp)
     for t in range(TILES):
         n = (t + 1) * QT
         f = t * QT
@@ -304,16 +314,6 @@
         rows = pl.ds(t * QT, QT)
         for h in range(HEADS):
             dq_out[rows, h * WIDTH : (h + 1) * WIDTH] = dq[:, h * QT : (h + 1) * QT].T.astype(dq_out.dtype)
-    for cp in summed:
-        cp.wait_recv()
-    some = pl.ds(pl.multiple_of(head * part + STRAIGHT, 16), part - STRAIGHT)
-    rest = prev_out[some, :].astype(jnp.float32)
-    for s in range(n_head - 1):
-        rest = rest + got_part[s].astype(jnp.float32)
-    rest_out[...] = rest.astype(jnp.bfloat16)
-    cp = copy_to(rest_out, got_rest, send_rest, recv_rest, before, head)
-    cp.start()
-    back.append(cp)
     for cp in back:
         cp.wait_recv()
     came = got_z[0].astype(jnp.float32)

time: 34.8 us -> 34.8 us (level)
  no operation moved by 1% of the time
where the time goes in v5:
time: 34.8 us; the launch traced here: 34.6 us
  Pallas kernels  34 us (98%)
  between operations  0.64 us (2%)
    pallas_call x1, Pallas kernels, shards(): pl.pallas_call(functools.partial(backward_kernel, n_ctx, n_head), out_sha...  33.2 us
    pallas_call x1, Pallas kernels, shards(): pl.pallas_call(hand_on_kernel, out_shape=tuple((jax.ShapeDtypeStruct(g.sh...  0.83 us

profile of v5, /device:TPU:1, one launch (start us, length us, event | category | flops | bytes accessed | tf_op | source)
XLA Modules:
  0.0 34.6 jit_solution(17797925636355120887)
XLA Ops:
  0.6 33.2 %backward.1 = (bf16[512,512]{1,0:T(8,128)(2,1)S(1)}, bf16[128,128]{1,0:T(8,128)(2,1)S(1)}, bf16[128,128]{1,0:T(8,128)(2,1)S(1)}) custom-call(s32[64]{0:T(128)} %seq_ref.1, s32[4,128]{1,0:T(4,128)} %bitcast.5, bf16[4,128,512]{2,1,0:T(8,128)(2,1)} %bitcast.3, bf16[512,128]{1,0:T(8,128)(2,1)} %k_hbm.1, bf16[512,128]{1,0:T(8,128)(2,1)} %v_hbm.1, ...), custom_call_target="tpu_custom_call" | custom-call | tf_op jit(solution)/shard_map/backward/pallas_call | solution.py:360
  33.8 0.8 %hand_on.1 = (bf16[512,512]{1,0:T(8,128)(2,1)}, bf16[128,128]{1,0:T(8,128)(2,1)}, bf16[128,128]{1,0:T(8,128)(2,1)}) custom-call(bf16[512,512]{1,0:T(8,128)(2,1)S(1)} %get-tuple-element.6.dq_ref, bf16[128,128]{1,0:T(8,128)(2,1)S(1)} %get-tuple-element.7.dk_ref, bf16[128,128]{1,0:T(8,128)(2,1)S(1)} %get-tuple-element.8.dv_ref), custom_call_target="tpu_custom_call" | custom-call | tf_op jit(solution)/shard_map/hand_on/pallas_call | solution.py:430

commit v6 on v5

--- a/solution.py
+++ b/solution.py
@@ -39,7 +39,7 @@
     dp = dot(v, do, 1, 1)
     m = jnp.max(s, axis=0, keepdims=True)
     if step > 0:
-        m_old = m_scr[step - 1, t]
+        m_old = m_scr[0 if step == CHUNKS else step + 1, t]
         m = jnp.maximum(m_old, m)
         shrink = jnp.exp2(m_old - m)
     p = jnp.exp2(s - m)
@@ -161,14 +161,14 @@
             loads.append(cp)
     pl.semaphore_wait(barrier, len(senders))
 
-    far = []
-    for r in range(CHUNKS):
+    far = {}
+    for r in reversed(range(CHUNKS)):
         for which, src in ((0, k_hbm), (1, v_hbm)):
             rows = pl.ds(r * QT, QT)
             i = 2 * r + which
             cp = copy_to(src.at[rows], kv.at[2 + core, which, rows], send_k.at[i], recv_k.at[i], after, head)
             cp.start()
-            far.append(cp)
+            far[i] = cp
     near = []
     for which, src in ((0, k_hbm), (1, v_hbm)):
         cp = copy_to(src, kv.at[1, which], send_p.at[which], recv_p.at[which], partner, head)
@@ -190,7 +190,7 @@
             p_own.at[t, pl.ds(0, n)], dp_own.at[t, pl.ds(0, n)], *stats,
         )
 
-    forwards = []
+    forwards = {}
 
     def pass_on(r):
         rows = pl.ds(r * QT, QT)
@@ -200,14 +200,14 @@
             place = kv.at[2 + core, which, rows]
             cp = copy_to(place, place, send_f.at[i], recv_f.at[i], partner, head)
             cp.start()
-            forwards.append(cp)
-
-    pass_on(0)
+            forwards[i] = cp
+
+    pass_on(CHUNKS - 1)
     for cp in near:
         cp.wait_recv()
-    for r in range(CHUNKS):
-        if r + 1 < CHUNKS:
-            pass_on(r + 1)
+    for r in reversed(range(CHUNKS)):
+        if r > 0:
+            pass_on(r - 1)
         rows = slice(r * QT, (r + 1) * QT)
         for which, dst in ((0, role_k), (1, role_v)):
             forwards[2 * r + which].wait_recv()
@@ -229,7 +229,7 @@
         l_scr[t] = inv
         d_scr[t] = d_scr[t] * inv
     for t in range(TILES):
-        factor = jnp.exp2(m_scr[1:, t] - m_scr[CHUNKS, t][None]) * l_scr[t][None]
+        factor = jnp.exp2(m_scr[1:, t] - m_scr[1, t][None]) * l_scr[t][None]
         dk, dv = key_grads(p_far[:, t, :QT], dp_far[:, t, :QT], factor, d_scr[t], qs[t], dos[t], ds_1.at[t])
         if t == 0:
             acc[1, :, :WIDTH] = dk
@@ -246,7 +246,7 @@
     trade.start()
     for t in range(TILES):
         f = t * QT
-        factor = jnp.exp2(m_scr[1 + t :, t] - m_scr[CHUNKS, t][None]) * l_scr[t][None]
+        factor = jnp.exp2(m_scr[1 + t :, t] - m_scr[1, t][None]) * l_scr[t][None]
         dk, dv = key_grads(
             p_far[t:, t, QT:], dp_far[t:, t, QT:], factor, d_scr[t], qs[t], dos[t], ds_2.at[t, pl.ds(f, ROWS - f)]
         )
@@ -276,7 +276,7 @@
         back.append(cp)
     for t in reversed(range(TILES)):
         n = (t + 1) * QT
-        factor = jnp.exp2(m_scr[0, t] - m_scr[CHUNKS, t]) * l_scr[t]
+        factor = jnp.exp2(m_scr[0, t] - m_scr[1, t]) * l_scr[t]
         dk, dv = key_grads(
             p_own[t, :n], dp_own[t, :n], factor, d_scr[t], qs[t], dos[t], ds_0.at[t, pl.ds(0, n)]
         )
@@ -333,7 +333,7 @@
     total = total + jnp.where(straight, came, swap_in[...].astype(jnp.float32))
     dk_ref[...] = total[:, :WIDTH].astype(jnp.bfloat16)
     dv_ref[...] = total[:, WIDTH:].astype(jnp.bfloat16)
-    for cp in far + near + forwards + [trade] + summed + back + across + [swap]:
+    for cp in list(far.values()) + near + list(forwards.values()) + [trade] + summed + back + across + [swap]:
         cp.wait_send()
 
 

time: 34.8 us -> 34.5 us (level)
  no operation moved by 1% of the time
where the time goes in v6:
time: 34.5 us; the launch traced here: 34.4 us
  Pallas kernels  33.7 us (98%)
  between operations  0.64 us (2%)
    pallas_call x1, Pallas kernels, shards(): pl.pallas_call(functools.partial(backward_kernel, n_ctx, n_head), out_sha...  32.9 us
    pallas_call x1, Pallas kernels, shards(): pl.pallas_call(hand_on_kernel, out_shape=tuple((jax.ShapeDtypeStruct(g.sh...  0.83 us

profile of v6, /device:TPU:1, one launch (start us, length us, event | category | flops | bytes accessed | tf_op | source)
XLA Modules:
  0.0 34.4 jit_solution(1155227913842894586)
XLA Ops:
  0.6 32.9 %backward.1 = (bf16[512,512]{1,0:T(8,128)(2,1)S(1)}, bf16[128,128]{1,0:T(8,128)(2,1)S(1)}, bf16[128,128]{1,0:T(8,128)(2,1)S(1)}) custom-call(s32[64]{0:T(128)} %seq_ref.1, s32[4,128]{1,0:T(4,128)} %bitcast.5, bf16[4,128,512]{2,1,0:T(8,128)(2,1)} %bitcast.3, bf16[512,128]{1,0:T(8,128)(2,1)} %k_hbm.1, bf16[512,128]{1,0:T(8,128)(2,1)} %v_hbm.1, ...), custom_call_target="tpu_custom_call" | custom-call | tf_op jit(solution)/shard_map/backward/pallas_call | solution.py:360
  33.5 0.8 %hand_on.1 = (bf16[512,512]{1,0:T(8,128)(2,1)}, bf16[128,128]{1,0:T(8,128)(2,1)}, bf16[128,128]{1,0:T(8,128)(2,1)}) custom-call(bf16[512,512]{1,0:T(8,128)(2,1)S(1)} %get-tuple-element.6.dq_ref, bf16[128,128]{1,0:T(8,128)(2,1)S(1)} %get-tuple-element.7.dk_ref, bf16[128,128]{1,0:T(8,128)(2,1)S(1)} %get-tuple-element.8.dv_ref), custom_call_target="tpu_custom_call" | custom-call | tf_op jit(solution)/shard_map/hand_on/pallas_call | solution.py:430
